TPU v7x, 256 devices: a whole 4x4x8 slice. The times are simulated.
256 devices in a mesh: group: 8 (over x, core), dp: 32 (over y, z).
Axes of the slice: x: 4, y: 4, z: 8, core: 2. Of those that a mesh axis runs over, the one named last changes fastest.
Arguments:
- latent_cache: bfloat16 [1024, 384, 512], P(('group', 'dp')), parts along dimension 0, may hold values from -17 to 17
- rope_cache: bfloat16 [1024, 64, 384], P(('group', 'dp')), parts along dimension 0, may hold values from -6 to 6
- q_latent: bfloat16 [8, 1024, 128, 512], P(None, ('group', 'dp')), parts along dimension 1, may hold values from -16 to 16
- q_rope: bfloat16 [8, 1024, 64, 128], P(None, ('group', 'dp')), parts along dimension 1, may hold values from -6 to 6
- new_latent: bfloat16 [8, 1024, 512], P(None, ('group', 'dp')), parts along dimension 1, may hold values from -6 to 6
- new_rope: bfloat16 [8, 1024, 64], P(None, ('group', 'dp')), parts along dimension 1, may hold values from -6 to 6
- req_length: int32 [1024], P('group'), parts along dimension 0, may hold values from 16 to 376, as said below
- req_dest: int32 [1024], P('group'), parts along dimension 0, may hold values from 0 to 31, as said below
Outputs:
- attention: bfloat16 [8, 1024, 128, 512], P(None, ('group', 'dp')), parts along dimension 1
- moved_latent: bfloat16 [1024, 384, 512], P(('group', 'dp')), parts along dimension 0
- moved_rope: bfloat16 [1024, 64, 384], P(('group', 'dp')), parts along dimension 0
There are 8 independent parts, one for each index of `group`. A program takes and returns all parts, laid end to end along the dimension named above; each array names one. Nothing has to cross between parts.
Inputs may be any that keep to these rules, and one draw needn't show every extreme that they name: Request r starts on rank r // 4 in slot r % 4 and goes to slot r % 4 of rank req_dest[r]. Every move is a swap of that slot between two ranks, so each rank holds 4 requests after the move; at most one request goes from one rank to another one, and in every draw some rank receives 4 requests from others. `req_length`: in every draw some request has exactly 376 cached tokens.
All inputs are finite; a program needn't handle non-finite values.
Results may differ from a plain program's by a relative error of at most 0.0048.
Values may be sent and summed in bfloat16 or wider, within the bound.
A program may use at most 128 MiB of HBM per device.

v0:
```python
import jax
import jax.numpy as jnp
from jax import lax
from jax.sharding import PartitionSpec as P

SCORE_SCALE = 192.0 ** (-0.5)


def body(latent_cache, rope_cache, q_latent, q_rope, new_latent, new_rope, req_length, req_dest):
    rank_total = lax.axis_size("dp")
    own_rank = lax.axis_index("dp")
    slot_count = latent_cache.shape[0]
    capacity = latent_cache.shape[1]
    step_count = q_latent.shape[0]
    dest_table = req_dest.reshape(rank_total, slot_count)
    rank_ids = jnp.arange(rank_total, dtype=jnp.int32)
    my_targets = lax.dynamic_index_in_dim(dest_table, own_rank, 0, keepdims=False)
    to_me = dest_table == own_rank
    staying = my_targets == own_rank
    lengths = jnp.sum(jnp.where(to_me, req_length.reshape(rank_total, slot_count), 0), axis=0)
    outgoing = (
        (my_targets[None, :] == rank_ids[:, None]) & (rank_ids[:, None] != own_rank)
    ).astype(jnp.bfloat16)
    send_latent = jnp.einsum(
        "dj,jlc->dlc", outgoing, latent_cache, preferred_element_type=jnp.bfloat16
    )
    send_rope = jnp.einsum("dj,jcl->dcl", outgoing, rope_cache, preferred_element_type=jnp.bfloat16)
    got_latent, got_rope = (
        lax.all_to_all(send_latent, "dp", split_axis=0, concat_axis=0, tiled=True),
        lax.all_to_all(send_rope, "dp", split_axis=0, concat_axis=0, tiled=True),
    )
    incoming = (to_me & (rank_ids[:, None] != own_rank)).astype(jnp.bfloat16)
    arrived_latent = jnp.einsum(
        "sj,slc->jlc", incoming, got_latent, preferred_element_type=jnp.bfloat16
    )
    arrived_rope = jnp.einsum(
        "sj,scl->jcl", incoming, got_rope, preferred_element_type=jnp.bfloat16
    )
    before_latent = jnp.where(staying[:, None, None], latent_cache, arrived_latent)
    before_rope = jnp.where(staying[:, None, None], rope_cache, arrived_rope)
    positions = jnp.arange(capacity, dtype=jnp.int32)
    step_ids = jnp.arange(step_count, dtype=jnp.int32)
    offsets = positions[None, :] - lengths[:, None]
    new_slot = (offsets[:, :, None] == step_ids[None, None, :]).astype(jnp.bfloat16)
    fresh_latent = jnp.einsum(
        "jlt,tjc->jlc", new_slot, new_latent, preferred_element_type=jnp.bfloat16
    )
    fresh_rope = jnp.einsum("jlt,tjc->jcl", new_slot, new_rope, preferred_element_type=jnp.bfloat16)
    resident = offsets < 0
    moved_latent = jnp.where(resident[:, :, None], before_latent, fresh_latent)
    moved_rope = jnp.where(resident[:, None, :], before_rope, fresh_rope)
    scores = (
        jnp.einsum("tjhc,jlc->jthl", q_latent, moved_latent, preferred_element_type=jnp.float32)
        + jnp.einsum("tjch,jcl->jthl", q_rope, moved_rope, preferred_element_type=jnp.float32)
    ) * SCORE_SCALE
    visible = positions[None, None, :] < lengths[:, None, None] + step_ids[None, :, None] + 1
    scores = jnp.where(visible[:, :, None, :], scores, -jnp.inf)
    row_max = jnp.max(scores, axis=-1, keepdims=True)
    raised = jnp.exp(scores - row_max)
    weights = (raised / jnp.sum(raised, axis=-1, keepdims=True)).astype(jnp.bfloat16)
    attention = jnp.einsum(
        "jthl,jlc->tjhc", weights, moved_latent, preferred_element_type=jnp.float32
    ).astype(jnp.bfloat16)
    return (attention, moved_latent, moved_rope)


def solution(mesh):
    return jax.shard_map(
        body,
        mesh=mesh,
        in_specs=(
            P(("group", "dp"), None, None),
            P(("group", "dp"), None, None),
            P(None, ("group", "dp"), None, None),
            P(None, ("group", "dp"), None, None),
            P(None, ("group", "dp"), None),
            P(None, ("group", "dp"), None),
            P("group"),
            P("group"),
        ),
        out_specs=(
            P(None, ("group", "dp"), None, None),
            P(("group", "dp"), None, None),
            P(("group", "dp"), None, None),
        ),
        check_vma=False,
    )
```

profile of v0, /device:TPU:173, one launch (start us, length us, event | category | flops | bytes accessed | tf_op | source)
XLA Modules:
  0.0 422.0 jit_solution(772425348026239564)
XLA Ops:
  0.6 0.0 copy-start
  0.7 0.9 reshape.109
  1.6 1.6 fusion.21
  3.2 1.7 copy.88
  4.9 8.9 %all-to-all-start.1 = ((bf16[32,64,384]{2,1,0:T(8,128)(2,1)}), bf16[32,64,384]{2,1,0:T(8,128)(2,1)}, u32[]{:S(2)}, u32[]{:S(2)}) async-start(bf16[32,64,384]{2,1,0:T(8,128)(2,1)} %copy.88), calls=%async_computation.1 | async-start | bytes 3145728 | tf_op jit(solution)/shard_map/all_to_all | solution.py:30
  13.9 3.9 fusion.9
  17.8 24.5 %copy.80 = bf16[32,384,512]{2,1,0:T(8,128)(2,1)} copy(bf16[32,384,512]{2,0,1:T(8,128)(2,1)S(1)} %fusion.9) | data formatting | bytes 25165824 | tf_op jit(solution)/shard_map/dj,jlc->dlc/dot_general | solution.py:24
  42.2 7.8 %all-to-all-done.1 = bf16[32,64,384]{2,1,0:T(8,128)(2,1)} async-done(((bf16[32,64,384]{2,1,0:T(8,128)(2,1)}), bf16[32,64,384]{2,1,0:T(8,128)(2,1)}, u32[]{:S(2)}, u32[]{:S(2)}) %all-to-all-start.1) | async-done | bytes 1572896 | tf_op jit(solution)/shard_map/all_to_all | solution.py:30
  50.0 8.4 %all-to-all-start = ((bf16[32,384,512]{2,1,0:T(8,128)(2,1)}), bf16[32,384,512]{2,1,0:T(8,128)(2,1)}, u32[]{:S(2)}, u32[]{:S(2)}) async-start(bf16[32,384,512]{2,1,0:T(8,128)(2,1)} %copy.80), calls=%async_computation | async-start | bytes 25165824 | tf_op jit(solution)/shard_map/all_to_all | solution.py:29
  58.4 0.1 copy.76
  58.5 0.1 reshape.110
  58.6 0.1 copy.77
  58.7 0.1 select_reduce_fusion
  58.8 0.1 broadcast_compare_fusion
  58.9 0.2 copy.78
  59.1 0.1 add_add_fusion
  59.2 0.1 iota_subtract_fusion
  59.2 0.1 iota_compare_fusion
  59.3 0.2 fusion.23
  59.6 1.8 fusion.24
  61.4 2.5 fusion.14
  63.8 0.7 copy.99
  64.5 297.7 %all-to-all-done = bf16[32,384,512]{2,1,0:T(8,128)(2,1)} async-done(((bf16[32,384,512]{2,1,0:T(8,128)(2,1)}), bf16[32,384,512]{2,1,0:T(8,128)(2,1)}, u32[]{:S(2)}, u32[]{:S(2)}) %all-to-all-start) | async-done | bytes 12582944 | tf_op jit(solution)/shard_map/all_to_all | solution.py:29
  362.3 29.4 %copy_select_fusion = bf16[4,384,512]{2,0,1:T(4,128)(2,1)S(1)} fusion(bf16[4,384,512]{2,1,0:T(8,128)(2,1)} %fusion.24, pred[4]{0:T(512)(128)(4,1)S(1)} %get-tuple-element.15, pred[4,384]{0,1:T(8,128)(4,1)S(1)} %copy.78, bf16[4,384,512]{2,1,0:T(8,128)(2,1)S(1)} %copy-done.3, bf16[32,384,512]{2,1,0:T(8,128)(2,1)} %all-to-all-done, ...), kind=kOutput, calls=%fused_computation.13 | convolution fusion | flops 51904640 | bytes 17303204 | tf_op jit(solution)/shard_map/sj,slc->jlc/dot_general | solution.py:33
  391.7 1.7 copy.98
  393.4 3.0 copy.102
  396.4 3.9 fusion.3
  400.3 2.5 bitcast_select_fusion
  402.7 2.6 copy-done.1
  405.4 1.1 fusion.40
  406.5 9.1 %convert_bitcast_fusion = bf16[8,4,128,512]{2,3,0,1:T(8,128)(2,1)} fusion(bf16[4,384,512,1]{1,2,3,0:T(8,128)(2,1)S(1)} %copy.102, f32[4,8,128]{2,1,0:T(8,128)S(1)} %fusion.40, f32[4,8,128,384]{2,3,1,0:T(8,128)} %copy-done.1), kind=kOutput, calls=%fused_computation.8 | convolution fusion | flops 1617432960 | bytes 12075008 | tf_op jit(solution)/shard_map/jthl,jlc->tjhc/dot_general | solution.py:61
  415.6 6.4 %copy.97 = bf16[8,4,128,512]{3,2,1,0:T(8,128)(2,1)} copy(bf16[8,4,128,512]{2,3,0,1:T(8,128)(2,1)} %convert_bitcast_fusion) | data formatting | bytes 8388608
  (16 shorter events, 0.1 us)
Async XLA Ops:
  0.6 399.6 %copy-start = (bf16[8,4,64,128]{3,2,1,0:T(8,128)(2,1)S(1)}, bf16[8,4,64,128]{3,2,1,0:T(8,128)(2,1)}, u32[]{:S(2)}) copy-start(bf16[8,4,64,128]{3,2,1,0:T(8,128)(2,1)} %param.11) | copy-start | bytes 1572868
  0.6 13.2 %copy-start.3 = (bf16[4,384,512]{2,1,0:T(8,128)(2,1)S(1)}, bf16[4,384,512]{2,1,0:T(8,128)(2,1)}, u32[]{:S(2)}) copy-start(bf16[4,384,512]{2,1,0:T(8,128)(2,1)} %param.8) | copy-start | bytes 4718596
  4.9 45.1 %all-to-all-start.1 = ((bf16[32,64,384]{2,1,0:T(8,128)(2,1)}), bf16[32,64,384]{2,1,0:T(8,128)(2,1)}, u32[]{:S(2)}, u32[]{:S(2)}) async-start(bf16[32,64,384]{2,1,0:T(8,128)(2,1)} %copy.88), calls=%async_computation.1 | async-start | bytes 3145728 | tf_op jit(solution)/shard_map/all_to_all | solution.py:30
  42.2 16.3 %copy-start.7 = (s32[128]{0:T(128)S(1)}, s32[128]{0:T(128)}, u32[]{:S(2)}) copy-start(s32[128]{0:T(128)} %param.14) | copy-start | bytes 1540
  42.2 17.1 %copy-start.6 = (bf16[8,4,64]{2,1,0:T(4,128)(2,1)S(1)}, bf16[8,4,64]{2,1,0:T(4,128)(2,1)}, u32[]{:S(2)}) copy-start(bf16[8,4,64]{2,1,0:T(4,128)(2,1)} %param.13) | copy-start | bytes 12292
  42.2 17.4 %copy-start.5 = (bf16[8,4,512]{2,1,0:T(4,128)(2,1)S(1)}, bf16[8,4,512]{2,1,0:T(4,128)(2,1)}, u32[]{:S(2)}) copy-start(bf16[8,4,512]{2,1,0:T(4,128)(2,1)} %param.12) | copy-start | bytes 98308
  42.2 19.1 %copy-start.4 = (bf16[4,64,384]{2,1,0:T(8,128)(2,1)S(1)}, bf16[4,64,384]{2,1,0:T(8,128)(2,1)}, u32[]{:S(2)}) copy-start(bf16[4,64,384]{2,1,0:T(8,128)(2,1)} %param.9) | copy-start | bytes 589828
  50.0 312.2 %all-to-all-start = ((bf16[32,384,512]{2,1,0:T(8,128)(2,1)}), bf16[32,384,512]{2,1,0:T(8,128)(2,1)}, u32[]{:S(2)}, u32[]{:S(2)}) async-start(bf16[32,384,512]{2,1,0:T(8,128)(2,1)} %copy.80), calls=%async_computation | async-start | bytes 25165824 | tf_op jit(solution)/shard_map/all_to_all | solution.py:29
  391.7 1.7 copy-start.2
  402.7 2.6 copy-start.1
where the time goes:
time: 423 us; the launch traced here: 422 us
  waiting for transfers between devices  306 us (72%)
  matrix products  54.8 us (13%)
  local copies, waits for them, and re-layouts  42 us (10%)
  starting transfers between devices  17.3 us (4%)
    all_to_all x1, waiting for transfers between devices, body(): lax.all_to_all(send_latent, 'dp', split_axis=0, concat_axis=0, tiled=True)  298 us
    dot_general x1, matrix products, body(): jnp.einsum('sj,slc->jlc', incoming, got_latent, preferred_element_type=jn...  29.4 us
    dot_general x1, local copies, waits for them, and re-layouts, body(): jnp.einsum('dj,jlc->dlc', outgoing, latent_cache, preferred_element_type=...  24.5 us
    unnamed x19, local copies, waits for them, and re-layouts  11.5 us
    dot_general x1, matrix products, body(): jnp.einsum('jthl,jlc->tjhc', weights, moved_latent, preferred_element_typ...  9.09 us
    all_to_all x1, starting transfers between devices, body(): lax.all_to_all(send_rope, 'dp', split_axis=0, concat_axis=0, tiled=True)  8.92 us
  transfers between devices with their start and end apart: 2, of which 2 were waited for; matrix products, arithmetic and copies ran while one was open for 8% of the time, Pallas kernels for 0%

commit v1 on v0

v1 whole, which is shorter than its diff:
```python
import math

import jax
import jax.numpy as jnp
from jax import lax
from jax.experimental import pallas as pl
from jax.experimental.pallas import tpu as pltpu
from jax.sharding import PartitionSpec as P

MESH = pl.DeviceIdType.MESH
RANKS = 32
RING = 8
SLOTS = 4
ROWS = 384
LATENT = 512
ROPE = 64
STEPS = 8
HEADS = 128
PIECE_ROWS = 48
TILE = 128
ROPE_UNITS = 12
LOG2E_SCALE = 192.0 ** (-0.5) * math.log2(math.e)


def shifted(rank, k):
    y, z = rank // RING, rank % RING
    return (y + k // RING) % 4 * RING + (z + 3 * k) % RING


def latent_piece(ref, slot, piece):
    row = pl.multiple_of(piece // 4 * PIECE_ROWS, PIECE_ROWS)
    column = pl.multiple_of(piece % 4 * TILE, TILE)
    return ref.at[slot, pl.ds(row, PIECE_ROWS), pl.ds(column, TILE)]


def rope_unit(ref, slot, unit):
    row = pl.multiple_of(unit % 4 * 16, 16)
    column = pl.multiple_of(unit // 4 * TILE, TILE)
    return ref.at[slot, pl.ds(row, 16), pl.ds(column, TILE)]


def exchange_kernel(
    dest_ref, latent_ref, rope_ref, out_latent, out_rope,
    held, staged, held_rope, staged_rope,
    send_one, recv_one, send_two, recv_two,
    send_one_rope, recv_one_rope, send_two_rope, recv_two_rope,
):
    me = lax.axis_index("dp")
    barrier = pltpu.get_barrier_semaphore()

    @pl.loop(1, RANKS)
    def _(k):
        pl.semaphore_signal(barrier, inc=1, device_id={"dp": shifted(me, k)}, device_id_type=MESH)

    pl.semaphore_wait(barrier, RANKS - 1)

    def rope_slot_of(u):
        return (me + RANKS * u) // ROPE_UNITS

    def send_rope(slot):
        @pl.loop(0, ROPE_UNITS)
        def _(i):
            q = (i + me) % ROPE_UNITS
            unit = slot * ROPE_UNITS + q
            peer, u = unit % RANKS, unit // RANKS
            source = rope_unit(rope_ref, slot, q)

            for w in range(2):
                if slot * ROPE_UNITS // RANKS <= w <= (slot * ROPE_UNITS + ROPE_UNITS - 1) // RANKS:
                    target = held_rope[w].at[me]

                    @pl.when((u == w) & (peer == me))
                    def _():
                        pltpu.make_async_copy(source, target, recv_one_rope.at[w]).start()

                    @pl.when((u == w) & (peer != me))
                    def _():
                        pltpu.make_async_remote_copy(
                            source, target, send_one_rope.at[slot], recv_one_rope.at[w],
                            device_id={"dp": peer}, device_id_type=MESH,
                        ).start()

    for slot in range(SLOTS):
        pltpu.make_async_copy(
            latent_piece(latent_ref, slot, me), held[slot].at[me], recv_one.at[slot]
        ).start()

        @pl.loop(1, RANKS)
        def _(k):
            peer = shifted(me, k)
            pltpu.make_async_remote_copy(
                latent_piece(latent_ref, slot, peer), held[slot].at[me],
                send_one.at[slot], recv_one.at[slot],
                device_id={"dp": peer}, device_id_type=MESH,
            ).start()

        send_rope(slot)

    def forward_rope(u):
        pltpu.make_async_copy(held_rope[u], held_rope[u], recv_one_rope.at[u]).wait()
        unit = me + RANKS * u
        slot, q = unit // ROPE_UNITS, unit % ROPE_UNITS

        @pl.loop(0, RANKS)
        def _(k):
            peer = shifted(me, k)
            origin = dest_ref[peer * SLOTS + slot]
            staged_rope[u, peer] = held_rope[u][origin]
            source, target = staged_rope.at[u, peer], rope_unit(out_rope, slot, q)

            @pl.when(k == 0)
            def _():
                pltpu.make_async_copy(source, target, recv_two_rope.at[slot]).start()

            @pl.when(k != 0)
            def _():
                pltpu.make_async_remote_copy(
                    source, target, send_two_rope.at[u], recv_two_rope.at[slot],
                    device_id={"dp": peer}, device_id_type=MESH,
                ).start()

    for slot in range(SLOTS):
        pltpu.make_async_copy(held[slot], held[slot], recv_one.at[slot]).wait()

        @pl.loop(0, RANKS)
        def _(k):
            peer = shifted(me, k)
            origin = dest_ref[peer * SLOTS + slot]
            staged[slot, peer] = held[slot][origin]
            source, target = staged.at[slot, peer], latent_piece(out_latent, slot, me)

            @pl.when(k == 0)
            def _():
                pltpu.make_async_copy(source, target, recv_two.at[slot]).start()

            @pl.when(k != 0)
            def _():
                pltpu.make_async_remote_copy(
                    source, target, send_two.at[slot], recv_two.at[slot],
                    device_id={"dp": peer}, device_id_type=MESH,
                ).start()

        if slot == 2:
            forward_rope(0)
        if slot == 3:
            pl.when(me < 16)(lambda: forward_rope(1))

    for slot in range(SLOTS):
        pltpu.make_async_copy(out_latent.at[slot], out_latent.at[slot], recv_two.at[slot]).wait()
        pltpu.make_async_copy(out_rope.at[slot], out_rope.at[slot], recv_two_rope.at[slot]).wait()

    others = pl.ds(0, RANKS - 1)
    for slot in range(SLOTS):
        pltpu.make_async_copy(held[slot].at[others], held[slot].at[others], send_one.at[slot]).wait()
        pltpu.make_async_copy(staged.at[slot, others], staged.at[slot, others], send_two.at[slot]).wait()
        own = (rope_slot_of(0) == slot) | ((me < 16) & (rope_slot_of(1) == slot))

        @pl.when(own)
        def _():
            part = held_rope[0].at[pl.ds(0, ROPE_UNITS - 1)]
            pltpu.make_async_copy(part, part, send_one_rope.at[slot]).wait()

        @pl.when(jnp.logical_not(own))
        def _():
            part = held_rope[0].at[pl.ds(0, ROPE_UNITS)]
            pltpu.make_async_copy(part, part, send_one_rope.at[slot]).wait()

    rest = staged_rope.at[0, pl.ds(0, RANKS - 1)]
    pltpu.make_async_copy(rest, rest, send_two_rope.at[0]).wait()

    @pl.when(me < 16)
    def _():
        pltpu.make_async_copy(rest, rest, send_two_rope.at[1]).wait()


def exchange(req_dest, latent_cache, rope_cache):
    anywhere = pl.BlockSpec(memory_space=pl.ANY)
    dma = pltpu.SemaphoreType.DMA
    return pl.pallas_call(
        exchange_kernel,
        out_shape=(
            jax.ShapeDtypeStruct(latent_cache.shape, jnp.bfloat16),
            jax.ShapeDtypeStruct(rope_cache.shape, jnp.bfloat16),
        ),
        in_specs=[pl.BlockSpec(memory_space=pltpu.SMEM), anywhere, anywhere],
        out_specs=(anywhere, anywhere),
        scratch_shapes=[
            (pltpu.VMEM((RANKS, PIECE_ROWS, TILE), jnp.bfloat16),) * SLOTS,
            pltpu.VMEM((SLOTS, RANKS, PIECE_ROWS, TILE), jnp.bfloat16),
            (pltpu.VMEM((RANKS, 16, TILE), jnp.bfloat16),) * 2,
            pltpu.VMEM((2, RANKS, 16, TILE), jnp.bfloat16),
            dma((SLOTS,)), dma((SLOTS,)), dma((SLOTS,)), dma((SLOTS,)),
            dma((SLOTS,)), dma((2,)), dma((2,)), dma((SLOTS,)),
        ],
        compiler_params=pltpu.CompilerParams(
            collective_id=0, has_side_effects=True, vmem_limit_bytes=16 * 2**20
        ),
        cost_estimate=pl.CostEstimate(flops=0, bytes_accessed=8 * 2**20, transcendentals=0),
        name="exchange",
    )(req_dest, latent_cache, rope_cache)


def attend_kernel(
    dest_ref, length_ref, latent_ref, rope_ref, q_ref, q_rope_ref, new_ref, new_rope_ref,
    out_ref, moved_ref, moved_rope_ref, fresh, fresh_rope,
):
    me = lax.axis_index("dp")
    slot = pl.program_id(0)
    length = length_ref[dest_ref[me * SLOTS + slot] * SLOTS + slot]

    for k in range(SLOTS):
        @pl.when(slot == k)
        def _():
            fresh[...] = new_ref[:, k, :]
            fresh_rope[...] = new_rope_ref[:, k, :]

    row = lax.broadcasted_iota(jnp.int32, (ROWS, STEPS), 0)
    step = lax.broadcasted_iota(jnp.int32, (ROWS, STEPS), 1)
    placed = jnp.where(row - length == step, 1.0, 0.0).astype(jnp.bfloat16)
    added = jnp.dot(placed, fresh[...], preferred_element_type=jnp.float32).astype(jnp.bfloat16)
    position = lax.broadcasted_iota(jnp.int32, (ROWS, LATENT), 0)
    keys = jnp.where(position < length, latent_ref[0], added)
    moved_ref[0] = keys

    added_rope = lax.dot_general(
        fresh_rope[...], placed, (((0,), (1,)), ((), ())), preferred_element_type=jnp.float32
    ).astype(jnp.bfloat16)
    position = lax.broadcasted_iota(jnp.int32, (ROPE, ROWS), 1)
    keys_rope = jnp.where(position < length, rope_ref[0], added_rope)
    moved_rope_ref[0] = keys_rope

    column = lax.broadcasted_iota(jnp.int32, (HEADS, ROWS), 1)
    for t in range(STEPS):
        scores = lax.dot_general(
            q_ref[t, 0], keys, (((1,), (1,)), ((), ())), preferred_element_type=jnp.float32
        ) + lax.dot_general(
            q_rope_ref[t, 0], keys_rope, (((0,), (0,)), ((), ())), preferred_element_type=jnp.float32
        )
        scores = jnp.where(column <= length + t, scores * LOG2E_SCALE, -jnp.inf)
        raised = jnp.exp2(scores - jnp.max(scores, axis=1, keepdims=True))
        total = jnp.sum(raised, axis=1, keepdims=True)
        result = jnp.dot(raised.astype(jnp.bfloat16), keys, preferred_element_type=jnp.float32)
        out_ref[t, 0] = (result * (1.0 / total)).astype(jnp.bfloat16)


def attend(req_dest, req_length, latent, rope, q_latent, q_rope, new_latent, new_rope):
    scalars = pl.BlockSpec(memory_space=pltpu.SMEM)
    by_slot = lambda *shape: pl.BlockSpec((1, *shape), lambda j: (j, 0, 0))
    by_step = lambda *shape: pl.BlockSpec((STEPS, 1, *shape), lambda j: (0, j, 0, 0))
    whole = lambda array: pl.BlockSpec(array.shape, lambda j: (0, 0, 0))
    return pl.pallas_call(
        attend_kernel,
        grid=(SLOTS,),
        out_shape=(
            jax.ShapeDtypeStruct(q_latent.shape, jnp.bfloat16),
            jax.ShapeDtypeStruct(latent.shape, jnp.bfloat16),
            jax.ShapeDtypeStruct(rope.shape, jnp.bfloat16),
        ),
        in_specs=[
            scalars, scalars, by_slot(ROWS, LATENT), by_slot(ROPE, ROWS),
            by_step(HEADS, LATENT), by_step(ROPE, HEADS), whole(new_latent), whole(new_rope),
        ],
        out_specs=(by_step(HEADS, LATENT), by_slot(ROWS, LATENT), by_slot(ROPE, ROWS)),
        scratch_shapes=[
            pltpu.VMEM((STEPS, LATENT), jnp.bfloat16),
            pltpu.VMEM((STEPS, ROPE), jnp.bfloat16),
        ],
        compiler_params=pltpu.CompilerParams(vmem_limit_bytes=32 * 2**20),
        cost_estimate=pl.CostEstimate(
            flops=3_500_000_000, bytes_accessed=12 * 2**20, transcendentals=1_600_000
        ),
        name="attend",
    )(req_dest, req_length, latent, rope, q_latent, q_rope, new_latent, new_rope)


def body(latent_cache, rope_cache, q_latent, q_rope, new_latent, new_rope, req_length, req_dest):
    latent, rope = exchange(req_dest, latent_cache, rope_cache)
    return attend(req_dest, req_length, latent, rope, q_latent, q_rope, new_latent, new_rope)


def solution(mesh):
    return jax.shard_map(
        body,
        mesh=mesh,
        in_specs=(
            P(("group", "dp"), None, None),
            P(("group", "dp"), None, None),
            P(None, ("group", "dp"), None, None),
            P(None, ("group", "dp"), None, None),
            P(None, ("group", "dp"), None),
            P(None, ("group", "dp"), None),
            P("group"),
            P("group"),
        ),
        out_specs=(
            P(None, ("group", "dp"), None, None),
            P(("group", "dp"), None, None),
            P(("group", "dp"), None, None),
        ),
        check_vma=False,
    )
```

time: 423 us -> 114 us (0.27)
  the two profiles are of different devices: /device:TPU:173 before, /device:TPU:1 now
where the time goes in v1:
time: 114 us
  Pallas kernels  108 us (95%)
  local copies, waits for them, and re-layouts  5.18 us (5%)
    pallas_call x1, Pallas kernels, exchange(): pl.pallas_call(exchange_kernel, out_shape=(jax.ShapeDtypeStruct(latent_ca...  90.9 us
    pallas_call x1, Pallas kernels, attend(): pl.pallas_call(attend_kernel, grid=(SLOTS,), out_shape=(jax.ShapeDtypeStr...  17.2 us
    unnamed x18, local copies, waits for them, and re-layouts  5.18 us

profile of v1, /device:TPU:1, one launch (start us, length us, event | category | flops | bytes accessed | tf_op | source)
XLA Modules:
  0.0 114.0 jit_solution(7287914706449536950)
XLA Ops:
  0.6 0.0 copy-start
  0.6 1.4 %copy-done = bf16[4,384,512]{2,1,0:T(8,128)(2,1)S(1)} copy-done((bf16[4,384,512]{2,1,0:T(8,128)(2,1)S(1)}, bf16[4,384,512]{2,1,0:T(8,128)(2,1)}, u32[]{:S(2)}) %copy-start) | copy-done | bytes 1572888
  2.0 0.0 copy-start.1
  2.0 0.9 copy-done.1
  3.0 0.0 copy-start.2
  3.0 0.7 copy-done.2
  3.6 0.0 copy-start.3
  3.6 0.0 copy-start.5
  3.6 0.0 copy-start.6
  3.6 0.0 copy-start.7
  3.6 0.0 copy-start.8
  3.6 90.9 %exchange.1 = (bf16[4,384,512]{2,1,0:T(8,128)(2,1)S(1)}, bf16[4,64,384]{2,1,0:T(8,128)(2,1)S(1)}) custom-call(s32[128]{0:T(128)S(1)} %copy-done.2, bf16[4,384,512]{2,1,0:T(8,128)(2,1)S(1)} %copy-done, bf16[4,64,384]{2,1,0:T(8,128)(2,1)S(1)} %copy-done.1), custom_call_target="tpu_custom_call" | custom-call | bytes 8388608 | tf_op jit(solution)/shard_map/exchange/pallas_call | solution.py:179
  94.6 0.0 copy-done.3
  94.6 0.0 copy-done.5
  94.6 0.0 copy-done.6
  94.6 0.0 copy-done.7
  94.6 0.0 copy-done.8
  94.6 0.0 copy-start.4
  94.6 2.2 %copy-done.4 = bf16[8,4,128,512]{3,2,1,0:T(8,128)(2,1)S(1)} copy-done((bf16[8,4,128,512]{3,2,1,0:T(8,128)(2,1)S(1)}, bf16[8,4,128,512]{3,2,1,0:T(8,128)(2,1)}, u32[]{:S(2)}) %copy-start.4) | copy-done | bytes 4194328
  96.8 17.2 %attend.1 = (bf16[8,4,128,512]{3,2,1,0:T(8,128)(2,1)}, bf16[4,384,512]{2,1,0:T(8,128)(2,1)}, bf16[4,64,384]{2,1,0:T(8,128)(2,1)}) custom-call(s32[128]{0:T(128)S(1)} %copy-done.3, s32[128]{0:T(128)S(1)} %copy-done.8, bf16[4,384,512]{2,1,0:T(8,128)(2,1)S(1)} %get-tuple-element.5.latent_ref, bf16[4,64,384]{2,1,0:T(8,128)(2,1)S(1)} %get-tuple-element.6.rope_ref, ...), custom_call_target="tpu_custom_call" | custom-call | flops 3500000000 | bytes 12582912 | tf_op jit(solution)/shard_map/attend/pallas_call | solution.py:251
Async XLA Ops:
  0.6 1.4 %copy-start = (bf16[4,384,512]{2,1,0:T(8,128)(2,1)S(1)}, bf16[4,384,512]{2,1,0:T(8,128)(2,1)}, u32[]{:S(2)}) copy-start(bf16[4,384,512]{2,1,0:T(8,128)(2,1)} %latent_ref.1) | copy-start | bytes 4718596
  2.0 0.9 copy-start.1
  3.0 0.7 copy-start.2
  3.6 90.9 %copy-start.3 = (s32[128]{0:T(128)S(1)}, s32[128]{0:T(128)}, u32[]{:S(2)}) copy-start(s32[128]{0:T(128)} %dest_ref.3) | copy-start | bytes 1540
  3.6 90.9 %copy-start.5 = (bf16[8,4,64,128]{3,2,1,0:T(8,128)(2,1)S(1)}, bf16[8,4,64,128]{3,2,1,0:T(8,128)(2,1)}, u32[]{:S(2)}) copy-start(bf16[8,4,64,128]{3,2,1,0:T(8,128)(2,1)} %q_rope_ref.1) | copy-start | bytes 1572868
  3.6 90.9 %copy-start.6 = (bf16[8,4,512]{2,1,0:T(4,128)(2,1)S(1)}, bf16[8,4,512]{2,1,0:T(4,128)(2,1)}, u32[]{:S(2)}) copy-start(bf16[8,4,512]{2,1,0:T(4,128)(2,1)} %new_ref.1) | copy-start | bytes 98308
  3.6 91.0 %copy-start.7 = (bf16[8,4,64]{2,1,0:T(4,128)(2,1)S(1)}, bf16[8,4,64]{2,1,0:T(4,128)(2,1)}, u32[]{:S(2)}) copy-start(bf16[8,4,64]{2,1,0:T(4,128)(2,1)} %new_rope_ref.1) | copy-start | bytes 12292
  3.6 91.0 %copy-start.8 = (s32[128]{0:T(128)S(1)}, s32[128]{0:T(128)}, u32[]{:S(2)}) copy-start(s32[128]{0:T(128)} %length_ref.1) | copy-start | bytes 1540
  94.6 2.2 %copy-start.4 = (bf16[8,4,128,512]{3,2,1,0:T(8,128)(2,1)S(1)}, bf16[8,4,128,512]{3,2,1,0:T(8,128)(2,1)}, u32[]{:S(2)}) copy-start(bf16[8,4,128,512]{3,2,1,0:T(8,128)(2,1)} %q_ref.1) | copy-start | bytes 12582916

commit v2 on v1

--- a/solution.py
+++ b/solution.py
@@ -193,7 +193,7 @@
             dma((SLOTS,)), dma((2,)), dma((2,)), dma((SLOTS,)),
         ],
         compiler_params=pltpu.CompilerParams(
-            collective_id=0, has_side_effects=True, vmem_limit_bytes=16 * 2**20
+            collective_id=0, has_side_effects=True, vmem_limit_bytes=60 * 2**20
         ),
         cost_estimate=pl.CostEstimate(flops=0, bytes_accessed=8 * 2**20, transcendentals=0),
         name="exchange",
@@ -229,18 +229,18 @@
     keys_rope = jnp.where(position < length, rope_ref[0], added_rope)
     moved_rope_ref[0] = keys_rope
 
-    column = lax.broadcasted_iota(jnp.int32, (HEADS, ROWS), 1)
-    for t in range(STEPS):
-        scores = lax.dot_general(
-            q_ref[t, 0], keys, (((1,), (1,)), ((), ())), preferred_element_type=jnp.float32
-        ) + lax.dot_general(
-            q_rope_ref[t, 0], keys_rope, (((0,), (0,)), ((), ())), preferred_element_type=jnp.float32
-        )
-        scores = jnp.where(column <= length + t, scores * LOG2E_SCALE, -jnp.inf)
-        raised = jnp.exp2(scores - jnp.max(scores, axis=1, keepdims=True))
-        total = jnp.sum(raised, axis=1, keepdims=True)
-        result = jnp.dot(raised.astype(jnp.bfloat16), keys, preferred_element_type=jnp.float32)
-        out_ref[t, 0] = (result * (1.0 / total)).astype(jnp.bfloat16)
+    shape = (STEPS, HEADS, ROWS)
+    seen = lax.broadcasted_iota(jnp.int32, shape, 2) <= length + lax.broadcasted_iota(jnp.int32, shape, 0)
+    queries = q_ref[:, 0].reshape(STEPS * HEADS, LATENT)
+    queries_rope = jnp.concatenate([q_rope_ref[t, 0].T for t in range(STEPS)], axis=0)
+    scores = lax.dot_general(
+        queries, moved_ref[0], (((1,), (1,)), ((), ())), preferred_element_type=jnp.float32
+    ) + jnp.dot(queries_rope, moved_rope_ref[0], preferred_element_type=jnp.float32)
+    scores = jnp.where(seen.reshape(STEPS * HEADS, ROWS), scores * LOG2E_SCALE, -jnp.inf)
+    raised = jnp.exp2(scores - jnp.max(scores, axis=1, keepdims=True))
+    total = jnp.sum(raised, axis=1, keepdims=True)
+    result = jnp.dot(raised.astype(jnp.bfloat16), moved_ref[0], preferred_element_type=jnp.float32)
+    out_ref[:, 0] = (result * (1.0 / total)).astype(jnp.bfloat16).reshape(STEPS, HEADS, LATENT)
 
 
 def attend(req_dest, req_length, latent, rope, q_latent, q_rope, new_latent, new_rope):
@@ -265,7 +265,7 @@
             pltpu.VMEM((STEPS, LATENT), jnp.bfloat16),
             pltpu.VMEM((STEPS, ROPE), jnp.bfloat16),
         ],
-        compiler_params=pltpu.CompilerParams(vmem_limit_bytes=32 * 2**20),
+        compiler_params=pltpu.CompilerParams(vmem_limit_bytes=60 * 2**20),
         cost_estimate=pl.CostEstimate(
             flops=3_500_000_000, bytes_accessed=12 * 2**20, transcendentals=1_600_000
         ),

time: 114 us -> 103 us (0.904)
  Pallas kernels: 108 us -> 102 us
  local copies, waits for them, and re-layouts: 5.18 us -> 0 us
    pallas_call x1, Pallas kernels: 17.2 us -> 10.2 us  [attend(): pl.pallas_call(attend_kernel, grid=(SLOTS,), out_shape=(jax.ShapeDtypeStr...]
    unnamed x18 -> x0, local copies, waits for them, and re-layouts: 5.18 us -> none
where the time goes in v2:
time: 103 us; the launch traced here: 102 us
  Pallas kernels  102 us (99%)
    pallas_call x1, Pallas kernels, exchange(): pl.pallas_call(exchange_kernel, out_shape=(jax.ShapeDtypeStruct(latent_ca...  91.3 us
    pallas_call x1, Pallas kernels, attend(): pl.pallas_call(attend_kernel, grid=(SLOTS,), out_shape=(jax.ShapeDtypeStr...  10.2 us

profile of v2, /device:TPU:1, one launch (start us, length us, event | category | flops | bytes accessed | tf_op | source)
XLA Modules:
  0.0 102.2 jit_solution(11042930241405168931)
XLA Ops:
  0.6 91.3 %exchange.1 = (bf16[4,384,512]{2,1,0:T(8,128)(2,1)}, bf16[4,64,384]{2,1,0:T(8,128)(2,1)}) custom-call(s32[128]{0:T(128)} %dest_ref.3, bf16[4,384,512]{2,1,0:T(8,128)(2,1)} %latent_ref.1, bf16[4,64,384]{2,1,0:T(8,128)(2,1)} %rope_ref.1), custom_call_target="tpu_custom_call" | custom-call | bytes 8388608 | tf_op jit(solution)/shard_map/exchange/pallas_call | solution.py:179
  92.0 10.2 %attend.1 = (bf16[8,4,128,512]{3,2,1,0:T(8,128)(2,1)}, bf16[4,384,512]{2,1,0:T(8,128)(2,1)}, bf16[4,64,384]{2,1,0:T(8,128)(2,1)}) custom-call(s32[128]{0:T(128)} %dest_ref.3, s32[128]{0:T(128)} %length_ref.1, bf16[4,384,512]{2,1,0:T(8,128)(2,1)} %get-tuple-element.5.latent_ref, bf16[4,64,384]{2,1,0:T(8,128)(2,1)} %get-tuple-element.6.rope_ref, ...), custom_call_target="tpu_custom_call" | custom-call | flops 3500000000 | bytes 12582912 | tf_op jit(solution)/shard_map/attend/pallas_call | solution.py:251

commit v3 on v2

v3 whole, which is shorter than its diff:
```python
import math

import jax
import jax.numpy as jnp
from jax import lax
from jax.experimental import pallas as pl
from jax.experimental.pallas import tpu as pltpu
from jax.sharding import PartitionSpec as P

MESH = pl.DeviceIdType.MESH
RANKS = 32
RING = 8
SLOTS = 4
ROWS = 384
LATENT = 512
ROPE = 64
STEPS = 8
HEADS = 128
PIECE_ROWS = 48
TILE = 128
ROPE_UNITS = 12
EARLY = 3
LOG2E_SCALE = 192.0 ** (-0.5) * math.log2(math.e)


def shifted(rank, k):
    y, z = rank // RING, rank % RING
    return (y + k // RING) % 4 * RING + (z + 3 * k) % RING


def rope_place(rank):
    y, z = rank // RING, rank % RING
    return (y + z) % 2 * 16 + y * 4 + z // 2


def rope_rank(place):
    half, y, z = place // 16, place % 16 // 4, place % 4
    return y * RING + 2 * z + (y + half) % 2


def latent_piece(ref, slot, piece):
    row = pl.multiple_of(piece // 4 * PIECE_ROWS, PIECE_ROWS)
    column = pl.multiple_of(piece % 4 * TILE, TILE)
    return ref.at[slot, pl.ds(row, PIECE_ROWS), pl.ds(column, TILE)]


def rope_unit(ref, slot, unit):
    row = pl.multiple_of(unit % 4 * 16, 16)
    column = pl.multiple_of(unit // 4 * TILE, TILE)
    return ref.at[slot, pl.ds(row, 16), pl.ds(column, TILE)]


def merged(length, latent, rope, fresh, fresh_rope):
    row = lax.broadcasted_iota(jnp.int32, (ROWS, STEPS), 0)
    step = lax.broadcasted_iota(jnp.int32, (ROWS, STEPS), 1)
    placed = jnp.where(row - length == step, 1.0, 0.0).astype(jnp.bfloat16)
    added = jnp.dot(placed, fresh, preferred_element_type=jnp.float32).astype(jnp.bfloat16)
    position = lax.broadcasted_iota(jnp.int32, (ROWS, LATENT), 0)
    added_rope = lax.dot_general(
        fresh_rope, placed, (((0,), (1,)), ((), ())), preferred_element_type=jnp.float32
    ).astype(jnp.bfloat16)
    position_rope = lax.broadcasted_iota(jnp.int32, (ROPE, ROWS), 1)
    return (
        jnp.where(position < length, latent, added),
        jnp.where(position_rope < length, rope, added_rope),
    )


def attention_of(length, keys_ref, keys_rope_ref, q, q_rope, first=0):
    steps = q.shape[0]
    shape = (steps, HEADS, ROWS)
    seen = lax.broadcasted_iota(jnp.int32, shape, 2) <= length + first + lax.broadcasted_iota(jnp.int32, shape, 0)
    queries_rope = jnp.concatenate([q_rope[t].T for t in range(steps)], axis=0)
    scores = lax.dot_general(
        q.reshape(steps * HEADS, LATENT), keys_ref[...], (((1,), (1,)), ((), ())),
        preferred_element_type=jnp.float32,
    ) + jnp.dot(queries_rope, keys_rope_ref[...], preferred_element_type=jnp.float32)
    scores = jnp.where(seen.reshape(steps * HEADS, ROWS), scores * LOG2E_SCALE, -jnp.inf)
    raised = jnp.exp2(scores - jnp.max(scores, axis=1, keepdims=True))
    total = jnp.sum(raised, axis=1, keepdims=True)
    result = jnp.dot(raised.astype(jnp.bfloat16), keys_ref[...], preferred_element_type=jnp.float32)
    return (result * (1.0 / total)).astype(jnp.bfloat16).reshape(steps, HEADS, LATENT)


def exchange_kernel(
    dest_ref, length_ref, latent_ref, rope_ref, q_ref, q_rope_ref, new_ref, new_rope_ref,
    out_latent, out_rope, out_early, out_moved, out_moved_rope,
    held, staged, held_rope, staged_rope,
    q_early, q_rope_early, arrived, arrived_rope, early, moved, moved_rope,
    send_one, recv_one, send_two, recv_two,
    send_one_rope, recv_one_rope, send_two_rope, recv_two_rope,
    load_sem, store_sem,
):
    me = lax.axis_index("dp")
    place = rope_place(me)
    barrier = pltpu.get_barrier_semaphore()

    @pl.loop(1, RANKS)
    def _(k):
        pl.semaphore_signal(barrier, inc=1, device_id={"dp": shifted(me, k)}, device_id_type=MESH)

    pl.semaphore_wait(barrier, RANKS - 1)

    def send_rope(slot):
        @pl.loop(0, ROPE_UNITS)
        def _(i):
            q = (i + me) % ROPE_UNITS
            unit = slot * ROPE_UNITS + q
            peer, u = rope_rank(unit % RANKS), unit // RANKS
            source = rope_unit(rope_ref, slot, q)

            for w in range(2):
                if slot * ROPE_UNITS // RANKS <= w <= (slot * ROPE_UNITS + ROPE_UNITS - 1) // RANKS:
                    target = held_rope[w].at[me]

                    @pl.when((u == w) & (peer == me))
                    def _():
                        pltpu.make_async_copy(source, target, recv_one_rope.at[w]).start()

                    @pl.when((u == w) & (peer != me))
                    def _():
                        pltpu.make_async_remote_copy(
                            source, target, send_one_rope.at[slot], recv_one_rope.at[w],
                            device_id={"dp": peer}, device_id_type=MESH,
                        ).start()

    for slot in range(SLOTS):
        pltpu.make_async_copy(
            latent_piece(latent_ref, slot, me), held[slot].at[me], recv_one.at[slot]
        ).start()

        @pl.loop(1, RANKS)
        def _(k):
            peer = shifted(me, k)
            pltpu.make_async_remote_copy(
                latent_piece(latent_ref, slot, peer), held[slot].at[me],
                send_one.at[slot], recv_one.at[slot],
                device_id={"dp": peer}, device_id_type=MESH,
            ).start()

        send_rope(slot)

    load_q = pltpu.make_async_copy(q_ref.at[:, pl.ds(0, EARLY)], q_early, load_sem.at[0])
    load_q_rope = pltpu.make_async_copy(q_rope_ref.at[:, pl.ds(0, EARLY)], q_rope_early, load_sem.at[1])
    load_q.start()
    load_q_rope.start()

    def forward_rope(u):
        pltpu.make_async_copy(held_rope[u], held_rope[u], recv_one_rope.at[u]).wait()
        unit = place + RANKS * u
        slot, q = unit // ROPE_UNITS, unit % ROPE_UNITS

        @pl.loop(0, RANKS)
        def _(k):
            peer = shifted(me, k)
            origin = dest_ref[peer * SLOTS + slot]
            staged_rope[u, peer] = held_rope[u][origin]
            source, target = staged_rope.at[u, peer], rope_unit(out_rope, slot, q)

            @pl.when(k == 0)
            def _():
                pltpu.make_async_copy(source, target, recv_two_rope.at[slot]).start()

            @pl.when(k != 0)
            def _():
                pltpu.make_async_remote_copy(
                    source, target, send_two_rope.at[u], recv_two_rope.at[slot],
                    device_id={"dp": peer}, device_id_type=MESH,
                ).start()

    for slot in range(SLOTS):
        pltpu.make_async_copy(held[slot], held[slot], recv_one.at[slot]).wait()

        @pl.loop(0, RANKS)
        def _(k):
            peer = shifted(me, k)
            origin = dest_ref[peer * SLOTS + slot]
            staged[slot, peer] = held[slot][origin]
            source, target = staged.at[slot, peer], latent_piece(out_latent, slot, me)

            @pl.when(k == 0)
            def _():
                pltpu.make_async_copy(source, target, recv_two.at[slot]).start()

            @pl.when(k != 0)
            def _():
                pltpu.make_async_remote_copy(
                    source, target, send_two.at[slot], recv_two.at[slot],
                    device_id={"dp": peer}, device_id_type=MESH,
                ).start()

        for u in range(2):
            first, last = slot * ROPE_UNITS - RANKS * u, slot * ROPE_UNITS + ROPE_UNITS - RANKS * u
            first, last = max(first, 0), min(last, RANKS if u == 0 else 16)
            if first < last:
                pl.when((place >= first) & (place < last))(lambda u=u: forward_rope(u))

    def arrive(slot):
        pltpu.make_async_copy(out_latent.at[slot], out_latent.at[slot], recv_two.at[slot]).wait()
        pltpu.make_async_copy(out_rope.at[slot], out_rope.at[slot], recv_two_rope.at[slot]).wait()

    def stores(slot):
        return [
            pltpu.make_async_copy(early.at[slot], out_early.at[slot], store_sem.at[0, slot]),
            pltpu.make_async_copy(moved.at[slot], out_moved.at[slot], store_sem.at[1, slot]),
            pltpu.make_async_copy(moved_rope.at[slot], out_moved_rope.at[slot], store_sem.at[2, slot]),
        ]

    load_q.wait()
    load_q_rope.wait()
    for slot in range(EARLY):
        arrive(slot)
        load = pltpu.make_async_copy(out_latent.at[slot], arrived, load_sem.at[2])
        load_rope = pltpu.make_async_copy(out_rope.at[slot], arrived_rope, load_sem.at[3])
        load.start()
        load_rope.start()
        load.wait()
        load_rope.wait()
        length = length_ref[dest_ref[me * SLOTS + slot] * SLOTS + slot]
        moved[slot], moved_rope[slot] = merged(
            length, arrived[...], arrived_rope[...], new_ref[:, slot, :], new_rope_ref[:, slot, :]
        )
        early[slot] = attention_of(
            length, moved.at[slot], moved_rope.at[slot], q_early[:, slot], q_rope_early[:, slot]
        )
        for copy in stores(slot):
            copy.start()

    others = pl.ds(0, RANKS - 1)
    for slot in range(SLOTS):
        pltpu.make_async_copy(held[slot].at[others], held[slot].at[others], send_one.at[slot]).wait()
        own = place // ROPE_UNITS == slot
        own |= (place < 16) & ((place + RANKS) // ROPE_UNITS == slot)

        @pl.when(own)
        def _():
            part = held_rope[0].at[pl.ds(0, ROPE_UNITS - 1)]
            pltpu.make_async_copy(part, part, send_one_rope.at[slot]).wait()

        @pl.when(jnp.logical_not(own))
        def _():
            part = held_rope[0].at[pl.ds(0, ROPE_UNITS)]
            pltpu.make_async_copy(part, part, send_one_rope.at[slot]).wait()

    for slot in range(EARLY):
        for copy in stores(slot):
            copy.wait()
    for slot in range(SLOTS):
        pltpu.make_async_copy(staged.at[slot, others], staged.at[slot, others], send_two.at[slot]).wait()

    rest = staged_rope.at[0, others]
    pltpu.make_async_copy(rest, rest, send_two_rope.at[0]).wait()

    @pl.when(place < 16)
    def _():
        pltpu.make_async_copy(rest, rest, send_two_rope.at[1]).wait()

    for slot in range(EARLY, SLOTS):
        arrive(slot)


HBM = pl.BlockSpec(memory_space=pltpu.HBM)
ANY = pl.BlockSpec(memory_space=pl.ANY)
SMEM = pl.BlockSpec(memory_space=pltpu.SMEM)
VMEM = pl.BlockSpec(memory_space=pltpu.VMEM)


def like(*shape):
    return jax.ShapeDtypeStruct(shape, jnp.bfloat16)


def buffer(*shape):
    return pltpu.VMEM(shape, jnp.bfloat16)


def exchange(req_dest, req_length, latent_cache, rope_cache, q_latent, q_rope, new_latent, new_rope):
    dma = pltpu.SemaphoreType.DMA
    return pl.pallas_call(
        exchange_kernel,
        out_shape=(
            like(SLOTS, ROWS, LATENT), like(SLOTS, ROPE, ROWS),
            like(EARLY, STEPS, HEADS, LATENT), like(EARLY, ROWS, LATENT), like(EARLY, ROPE, ROWS),
        ),
        in_specs=[SMEM, SMEM, HBM, HBM, HBM, HBM, VMEM, VMEM],
        out_specs=(ANY,) * 5,
        scratch_shapes=[
            (buffer(RANKS, PIECE_ROWS, TILE),) * SLOTS,
            buffer(SLOTS, RANKS, PIECE_ROWS, TILE),
            (buffer(RANKS, 16, TILE),) * 2,
            buffer(2, RANKS, 16, TILE),
            buffer(STEPS, EARLY, HEADS, LATENT), buffer(STEPS, EARLY, ROPE, HEADS),
            buffer(ROWS, LATENT), buffer(ROPE, ROWS),
            buffer(EARLY, STEPS, HEADS, LATENT), buffer(EARLY, ROWS, LATENT), buffer(EARLY, ROPE, ROWS),
            dma((SLOTS,)), dma((SLOTS,)), dma((SLOTS,)), dma((SLOTS,)),
            dma((SLOTS,)), dma((2,)), dma((2,)), dma((SLOTS,)),
            dma((4,)), dma((3, EARLY)),
        ],
        compiler_params=pltpu.CompilerParams(
            collective_id=0, has_side_effects=True, vmem_limit_bytes=60 * 2**20
        ),
        cost_estimate=pl.CostEstimate(
            flops=2_600_000_000, bytes_accessed=16 * 2**20, transcendentals=1_200_000
        ),
        name="exchange",
    )(req_dest, req_length, latent_cache, rope_cache, q_latent, q_rope, new_latent, new_rope)


def finish_kernel(
    dest_ref, length_ref, latent_ref, rope_ref, early_ref, moved_ref, moved_rope_ref,
    q_ref, q_rope_ref, new_ref, new_rope_ref,
    out_ref, out_moved, out_moved_rope,
    latent, rope, q, q_rope, result, keys, keys_rope, early, moved, moved_rope, load_sem, store_sem,
):
    slot = EARLY
    loads = [
        pltpu.make_async_copy(latent_ref.at[slot], latent, load_sem.at[0]),
        pltpu.make_async_copy(rope_ref.at[slot], rope, load_sem.at[1]),
        pltpu.make_async_copy(q_ref.at[:, slot], q, load_sem.at[2]),
        pltpu.make_async_copy(q_rope_ref.at[:, slot], q_rope, load_sem.at[3]),
    ]
    for copy in loads:
        copy.start()
    fetches = [
        pltpu.make_async_copy(early_ref, early, load_sem.at[4]),
        pltpu.make_async_copy(moved_ref, moved, load_sem.at[5]),
        pltpu.make_async_copy(moved_rope_ref, moved_rope, load_sem.at[6]),
    ]
    copies = [
        pltpu.make_async_copy(early.at[k], out_ref.at[:, k], store_sem.at[k]) for k in range(EARLY)
    ] + [
        pltpu.make_async_copy(moved, out_moved.at[pl.ds(0, EARLY)], store_sem.at[EARLY]),
        pltpu.make_async_copy(moved_rope, out_moved_rope.at[pl.ds(0, EARLY)], store_sem.at[EARLY + 1]),
    ]
    for copy in fetches:
        copy.start()
    me = lax.axis_index("dp")
    length = length_ref[dest_ref[me * SLOTS + slot] * SLOTS + slot]
    loads[0].wait()
    loads[1].wait()
    keys[...], keys_rope[...] = merged(
        length, latent[...], rope[...], new_ref[:, slot, :], new_rope_ref[:, slot, :]
    )
    half = STEPS // 2
    own = [
        pltpu.make_async_copy(keys, out_moved.at[slot], store_sem.at[EARLY + 2]),
        pltpu.make_async_copy(keys_rope, out_moved_rope.at[slot], store_sem.at[EARLY + 3]),
    ] + [
        pltpu.make_async_copy(
            result.at[pl.ds(first, half)], out_ref.at[pl.ds(first, half), slot],
            store_sem.at[EARLY + 4 + first // half],
        )
        for first in (0, half)
    ]
    own[0].start()
    own[1].start()
    loads[2].wait()
    loads[3].wait()
    result[:half] = attention_of(length, keys, keys_rope, q[:half], q_rope[:half])
    own[2].start()
    for copy in fetches:
        copy.wait()
    for copy in copies:
        copy.start()
    result[half:] = attention_of(length, keys, keys_rope, q[half:], q_rope[half:], half)
    own[3].start()
    for copy in copies + own:
        copy.wait()


def finish(req_dest, req_length, exchanged, q_latent, q_rope, new_latent, new_rope):
    dma = pltpu.SemaphoreType.DMA
    return pl.pallas_call(
        finish_kernel,
        out_shape=(
            like(STEPS, SLOTS, HEADS, LATENT), like(SLOTS, ROWS, LATENT), like(SLOTS, ROPE, ROWS),
        ),
        in_specs=[SMEM, SMEM] + [ANY] * 5 + [HBM, HBM, VMEM, VMEM],
        out_specs=(HBM,) * 3,
        scratch_shapes=[
            buffer(ROWS, LATENT), buffer(ROPE, ROWS),
            buffer(STEPS, HEADS, LATENT), buffer(STEPS, ROPE, HEADS),
            buffer(STEPS, HEADS, LATENT), buffer(ROWS, LATENT), buffer(ROPE, ROWS),
            buffer(EARLY, STEPS, HEADS, LATENT), buffer(EARLY, ROWS, LATENT), buffer(EARLY, ROPE, ROWS),
            dma((7,)), dma((EARLY + 6,)),
        ],
        compiler_params=pltpu.CompilerParams(vmem_limit_bytes=60 * 2**20),
        cost_estimate=pl.CostEstimate(
            flops=900_000_000, bytes_accessed=12 * 2**20, transcendentals=400_000
        ),
        name="finish",
    )(req_dest, req_length, *exchanged, q_latent, q_rope, new_latent, new_rope)


def body(latent_cache, rope_cache, q_latent, q_rope, new_latent, new_rope, req_length, req_dest):
    queries = (q_latent, q_rope, new_latent, new_rope)
    exchanged = exchange(req_dest, req_length, latent_cache, rope_cache, *queries)
    return finish(req_dest, req_length, exchanged, *queries)


def solution(mesh):
    return jax.shard_map(
        body,
        mesh=mesh,
        in_specs=(
            P(("group", "dp"), None, None),
            P(("group", "dp"), None, None),
            P(None, ("group", "dp"), None, None),
            P(None, ("group", "dp"), None, None),
            P(None, ("group", "dp"), None),
            P(None, ("group", "dp"), None),
            P("group"),
            P("group"),
        ),
        out_specs=(
            P(None, ("group", "dp"), None, None),
            P(("group", "dp"), None, None),
            P(("group", "dp"), None, None),
        ),
        check_vma=False,
    )
```

time: 103 us -> 98.2 us (0.953)
  Pallas kernels: 102 us -> 97.3 us
    pallas_call x2, Pallas kernels: 102 us -> 97.3 us  [the longest x1 91.2 us: exchange(): pl.pallas_call(exchange_kernel, out_shape=(like(SLOTS, ROWS, LATENT), lik...]
where the time goes in v3:
time: 98.2 us; the launch traced here: 97.9 us
  Pallas kernels  97.3 us (99%)
    pallas_call x1, Pallas kernels, exchange(): pl.pallas_call(exchange_kernel, out_shape=(like(SLOTS, ROWS, LATENT), lik...  91.2 us
    pallas_call x1, Pallas kernels, finish(): pl.pallas_call(finish_kernel, out_shape=(like(STEPS, SLOTS, HEADS, LATENT...  6.07 us

profile of v3, /device:TPU:1, one launch (start us, length us, event | category | flops | bytes accessed | tf_op | source)
XLA Modules:
  0.0 97.9 jit_solution(9206464115180785415)
XLA Ops:
  0.6 91.2 %exchange.1 = (bf16[4,384,512]{2,1,0:T(8,128)(2,1)}, bf16[4,64,384]{2,1,0:T(8,128)(2,1)}, bf16[3,8,128,512]{3,2,1,0:T(8,128)(2,1)}, bf16[3,384,512]{2,1,0:T(8,128)(2,1)}, bf16[3,64,384]{2,1,0:T(8,128)(2,1)}) custom-call(s32[128]{0:T(128)} %dest_ref.3, s32[128]{0:T(128)} %length_ref.3, bf16[4,384,512]{2,1,0:T(8,128)(2,1)} %latent_ref.1, ...), custom_call_target="tpu_custom_call" | custom-call | flops 2600000000 | bytes 16777216 | tf_op jit(solution)/shard_map/exchange/pallas_call | solution.py:278
  91.9 6.1 %finish.1 = (bf16[8,4,128,512]{3,2,1,0:T(8,128)(2,1)}, bf16[4,384,512]{2,1,0:T(8,128)(2,1)}, bf16[4,64,384]{2,1,0:T(8,128)(2,1)}) custom-call(s32[128]{0:T(128)} %dest_ref.3, s32[128]{0:T(128)} %length_ref.3, bf16[4,384,512]{2,1,0:T(8,128)(2,1)} %get-tuple-element.8.latent_ref, bf16[4,64,384]{2,1,0:T(8,128)(2,1)} %get-tuple-element.9.rope_ref, ...), custom_call_target="tpu_custom_call" | custom-call | flops 900000000 | bytes 12582912 | tf_op jit(solution)/shard_map/finish/pallas_call | solution.py:372

commit v4 on v3

--- a/solution.py
+++ b/solution.py
@@ -66,15 +66,18 @@
     )
 
 
+def turned(q_rope):
+    return jnp.concatenate([q_rope[t].T for t in range(STEPS)], axis=0)
+
+
 def attention_of(length, keys_ref, keys_rope_ref, q, q_rope, first=0):
     steps = q.shape[0]
     shape = (steps, HEADS, ROWS)
     seen = lax.broadcasted_iota(jnp.int32, shape, 2) <= length + first + lax.broadcasted_iota(jnp.int32, shape, 0)
-    queries_rope = jnp.concatenate([q_rope[t].T for t in range(steps)], axis=0)
     scores = lax.dot_general(
         q.reshape(steps * HEADS, LATENT), keys_ref[...], (((1,), (1,)), ((), ())),
         preferred_element_type=jnp.float32,
-    ) + jnp.dot(queries_rope, keys_rope_ref[...], preferred_element_type=jnp.float32)
+    ) + jnp.dot(q_rope, keys_rope_ref[...], preferred_element_type=jnp.float32)
     scores = jnp.where(seen.reshape(steps * HEADS, ROWS), scores * LOG2E_SCALE, -jnp.inf)
     raised = jnp.exp2(scores - jnp.max(scores, axis=1, keepdims=True))
     total = jnp.sum(raised, axis=1, keepdims=True)
@@ -84,9 +87,9 @@
 
 def exchange_kernel(
     dest_ref, length_ref, latent_ref, rope_ref, q_ref, q_rope_ref, new_ref, new_rope_ref,
-    out_latent, out_rope, out_early, out_moved, out_moved_rope,
+    out_latent, out_rope, out_early, out_moved, out_moved_rope, out_q, out_q_rope,
     held, staged, held_rope, staged_rope,
-    q_early, q_rope_early, arrived, arrived_rope, early, moved, moved_rope,
+    q_early, q_rope_all, q_turned, arrived, arrived_rope, early, moved, moved_rope,
     send_one, recv_one, send_two, recv_two,
     send_one_rope, recv_one_rope, send_two_rope, recv_two_rope,
     load_sem, store_sem,
@@ -141,7 +144,9 @@
         send_rope(slot)
 
     load_q = pltpu.make_async_copy(q_ref.at[:, pl.ds(0, EARLY)], q_early, load_sem.at[0])
-    load_q_rope = pltpu.make_async_copy(q_rope_ref.at[:, pl.ds(0, EARLY)], q_rope_early, load_sem.at[1])
+    load_q_rope = pltpu.make_async_copy(q_rope_ref, q_rope_all, load_sem.at[1])
+    load_last = pltpu.make_async_copy(q_ref.at[:, EARLY], out_q, load_sem.at[4])
+    load_last.start()
     load_q.start()
     load_q_rope.start()
 
@@ -208,6 +213,9 @@
 
     load_q.wait()
     load_q_rope.wait()
+    q_turned[...] = turned(q_rope_all[:, EARLY])
+    store_turned = pltpu.make_async_copy(q_turned, out_q_rope, load_sem.at[5])
+    store_turned.start()
     for slot in range(EARLY):
         arrive(slot)
         load = pltpu.make_async_copy(out_latent.at[slot], arrived, load_sem.at[2])
@@ -221,7 +229,7 @@
             length, arrived[...], arrived_rope[...], new_ref[:, slot, :], new_rope_ref[:, slot, :]
         )
         early[slot] = attention_of(
-            length, moved.at[slot], moved_rope.at[slot], q_early[:, slot], q_rope_early[:, slot]
+            length, moved.at[slot], moved_rope.at[slot], q_early[:, slot], turned(q_rope_all[:, slot])
         )
         for copy in stores(slot):
             copy.start()
@@ -242,6 +250,8 @@
             part = held_rope[0].at[pl.ds(0, ROPE_UNITS)]
             pltpu.make_async_copy(part, part, send_one_rope.at[slot]).wait()
 
+    load_last.wait()
+    store_turned.wait()
     for slot in range(EARLY):
         for copy in stores(slot):
             copy.wait()
@@ -278,25 +288,27 @@
     return pl.pallas_call(
         exchange_kernel,
         out_shape=(
-            like(SLOTS, ROWS, LATENT), like(SLOTS, ROPE, ROWS),
-            like(EARLY, STEPS, HEADS, LATENT), like(EARLY, ROWS, LATENT), like(EARLY, ROPE, ROWS),
+            buffer(SLOTS, ROWS, LATENT), buffer(SLOTS, ROPE, ROWS),
+            buffer(EARLY, STEPS, HEADS, LATENT), buffer(EARLY, ROWS, LATENT), buffer(EARLY, ROPE, ROWS),
+            buffer(STEPS, HEADS, LATENT), buffer(STEPS * HEADS, ROPE),
         ),
         in_specs=[SMEM, SMEM, HBM, HBM, HBM, HBM, VMEM, VMEM],
-        out_specs=(ANY,) * 5,
+        out_specs=(ANY,) * 7,
         scratch_shapes=[
             (buffer(RANKS, PIECE_ROWS, TILE),) * SLOTS,
             buffer(SLOTS, RANKS, PIECE_ROWS, TILE),
             (buffer(RANKS, 16, TILE),) * 2,
             buffer(2, RANKS, 16, TILE),
-            buffer(STEPS, EARLY, HEADS, LATENT), buffer(STEPS, EARLY, ROPE, HEADS),
+            buffer(STEPS, EARLY, HEADS, LATENT), buffer(STEPS, SLOTS, ROPE, HEADS),
+            buffer(STEPS * HEADS, ROPE),
             buffer(ROWS, LATENT), buffer(ROPE, ROWS),
             buffer(EARLY, STEPS, HEADS, LATENT), buffer(EARLY, ROWS, LATENT), buffer(EARLY, ROPE, ROWS),
             dma((SLOTS,)), dma((SLOTS,)), dma((SLOTS,)), dma((SLOTS,)),
             dma((SLOTS,)), dma((2,)), dma((2,)), dma((SLOTS,)),
-            dma((4,)), dma((3, EARLY)),
+            dma((6,)), dma((3, EARLY)),
         ],
         compiler_params=pltpu.CompilerParams(
-            collective_id=0, has_side_effects=True, vmem_limit_bytes=60 * 2**20
+            collective_id=0, has_side_effects=True, vmem_limit_bytes=32 * 2**20
         ),
         cost_estimate=pl.CostEstimate(
             flops=2_600_000_000, bytes_accessed=16 * 2**20, transcendentals=1_200_000
@@ -307,31 +319,24 @@
 
 def finish_kernel(
     dest_ref, length_ref, latent_ref, rope_ref, early_ref, moved_ref, moved_rope_ref,
-    q_ref, q_rope_ref, new_ref, new_rope_ref,
+    q, q_rope, new_ref, new_rope_ref,
     out_ref, out_moved, out_moved_rope,
-    latent, rope, q, q_rope, result, keys, keys_rope, early, moved, moved_rope, load_sem, store_sem,
+    latent, rope, result, keys, keys_rope, load_sem, store_sem,
 ):
     slot = EARLY
     loads = [
         pltpu.make_async_copy(latent_ref.at[slot], latent, load_sem.at[0]),
         pltpu.make_async_copy(rope_ref.at[slot], rope, load_sem.at[1]),
-        pltpu.make_async_copy(q_ref.at[:, slot], q, load_sem.at[2]),
-        pltpu.make_async_copy(q_rope_ref.at[:, slot], q_rope, load_sem.at[3]),
     ]
     for copy in loads:
         copy.start()
-    fetches = [
-        pltpu.make_async_copy(early_ref, early, load_sem.at[4]),
-        pltpu.make_async_copy(moved_ref, moved, load_sem.at[5]),
-        pltpu.make_async_copy(moved_rope_ref, moved_rope, load_sem.at[6]),
+    copies = [
+        pltpu.make_async_copy(early_ref.at[k], out_ref.at[:, k], store_sem.at[k]) for k in range(EARLY)
+    ] + [
+        pltpu.make_async_copy(moved_ref, out_moved.at[pl.ds(0, EARLY)], store_sem.at[EARLY]),
+        pltpu.make_async_copy(moved_rope_ref, out_moved_rope.at[pl.ds(0, EARLY)], store_sem.at[EARLY + 1]),
     ]
-    copies = [
-        pltpu.make_async_copy(early.at[k], out_ref.at[:, k], store_sem.at[k]) for k in range(EARLY)
-    ] + [
-        pltpu.make_async_copy(moved, out_moved.at[pl.ds(0, EARLY)], store_sem.at[EARLY]),
-        pltpu.make_async_copy(moved_rope, out_moved_rope.at[pl.ds(0, EARLY)], store_sem.at[EARLY + 1]),
-    ]
-    for copy in fetches:
+    for copy in copies:
         copy.start()
     me = lax.axis_index("dp")
     length = length_ref[dest_ref[me * SLOTS + slot] * SLOTS + slot]
@@ -353,48 +358,42 @@
     ]
     own[0].start()
     own[1].start()
-    loads[2].wait()
-    loads[3].wait()
-    result[:half] = attention_of(length, keys, keys_rope, q[:half], q_rope[:half])
+    result[:half] = attention_of(length, keys, keys_rope, q[:half], q_rope[: half * HEADS])
     own[2].start()
-    for copy in fetches:
-        copy.wait()
-    for copy in copies:
-        copy.start()
-    result[half:] = attention_of(length, keys, keys_rope, q[half:], q_rope[half:], half)
+    result[half:] = attention_of(length, keys, keys_rope, q[half:], q_rope[half * HEADS :], half)
     own[3].start()
     for copy in copies + own:
         copy.wait()
 
 
-def finish(req_dest, req_length, exchanged, q_latent, q_rope, new_latent, new_rope):
+def finish(req_dest, req_length, exchanged, new_latent, new_rope):
     dma = pltpu.SemaphoreType.DMA
     return pl.pallas_call(
         finish_kernel,
         out_shape=(
             like(STEPS, SLOTS, HEADS, LATENT), like(SLOTS, ROWS, LATENT), like(SLOTS, ROPE, ROWS),
         ),
-        in_specs=[SMEM, SMEM] + [ANY] * 5 + [HBM, HBM, VMEM, VMEM],
+        in_specs=[SMEM, SMEM] + [ANY] * 5 + [VMEM] * 4,
         out_specs=(HBM,) * 3,
         scratch_shapes=[
             buffer(ROWS, LATENT), buffer(ROPE, ROWS),
-            buffer(STEPS, HEADS, LATENT), buffer(STEPS, ROPE, HEADS),
             buffer(STEPS, HEADS, LATENT), buffer(ROWS, LATENT), buffer(ROPE, ROWS),
-            buffer(EARLY, STEPS, HEADS, LATENT), buffer(EARLY, ROWS, LATENT), buffer(EARLY, ROPE, ROWS),
-            dma((7,)), dma((EARLY + 6,)),
+            dma((2,)), dma((EARLY + 6,)),
         ],
-        compiler_params=pltpu.CompilerParams(vmem_limit_bytes=60 * 2**20),
+        compiler_params=pltpu.CompilerParams(vmem_limit_bytes=20 * 2**20),
         cost_estimate=pl.CostEstimate(
             flops=900_000_000, bytes_accessed=12 * 2**20, transcendentals=400_000
         ),
         name="finish",
-    )(req_dest, req_length, *exchanged, q_latent, q_rope, new_latent, new_rope)
+    )(req_dest, req_length, *exchanged, new_latent, new_rope)
 
 
 def body(latent_cache, rope_cache, q_latent, q_rope, new_latent, new_rope, req_length, req_dest):
-    queries = (q_latent, q_rope, new_latent, new_rope)
+    in_hbm = lambda array: pltpu.with_memory_space_constraint(array, pltpu.HBM)
+    latent_cache, rope_cache, req_dest, req_length = map(in_hbm, (latent_cache, rope_cache, req_dest, req_length))
+    queries = tuple(map(in_hbm, (q_latent, q_rope, new_latent, new_rope)))
     exchanged = exchange(req_dest, req_length, latent_cache, rope_cache, *queries)
-    return finish(req_dest, req_length, exchanged, *queries)
+    return finish(req_dest, req_length, exchanged, *queries[2:])
 
 
 def solution(mesh):

time: 98.2 us -> 95.9 us (0.977)
  Pallas kernels: 97.3 us -> 95.1 us
    pallas_call x1, Pallas kernels: 6.07 us -> 3.92 us  [finish(): pl.pallas_call(finish_kernel, out_shape=(like(STEPS, SLOTS, HEADS, LATENT...]
where the time goes in v4:
time: 95.9 us; the launch traced here: 95.7 us
  Pallas kernels  95.1 us (99%)
    pallas_call x1, Pallas kernels, exchange(): pl.pallas_call(exchange_kernel, out_shape=(buffer(SLOTS, ROWS, LATENT), b...  91.2 us
    pallas_call x1, Pallas kernels, finish(): pl.pallas_call(finish_kernel, out_shape=(like(STEPS, SLOTS, HEADS, LATENT...  3.92 us

profile of v4, /device:TPU:1, one launch (start us, length us, event | category | flops | bytes accessed | tf_op | source)
XLA Modules:
  0.0 95.7 jit_solution(5345424352667167503)
XLA Ops:
  0.6 91.2 %exchange.1 = (bf16[4,384,512]{2,1,0:T(8,128)(2,1)S(1)}, bf16[4,64,384]{2,1,0:T(8,128)(2,1)S(1)}, bf16[3,8,128,512]{3,2,1,0:T(8,128)(2,1)S(1)}, bf16[3,384,512]{...) custom-call(s32[128]{0:T(128)} %dest_ref.3, ...), custom_call_target="tpu_custom_call" | custom-call | flops 2600000000 | bytes 16777216 | tf_op jit(solution)/shard_map/exchange/pallas_call | solution.py:288
  91.8 3.9 %finish.1 = (bf16[8,4,128,512]{3,2,1,0:T(8,128)(2,1)}, bf16[4,384,512]{2,1,0:T(8,128)(2,1)}, bf16[4,64,384]{2,1,0:T(8,128)(2,1)}) custom-call(s32[128]{0:T(128)} %dest_ref.3, s32[128]{0:T(128)} %length_ref.3, bf16[4,384,512]{2,1,0:T(8,128)(2,1)S(1)} %get-tuple-element.10.latent_ref, bf16[4,64,384]{2,1,0:T(8,128)(2,1)S(1)} %get-tuple-element.11.rope_ref, ...), custom_call_target="tpu_custom_call" | custom-call | flops 900000000 | bytes 12582912 | tf_op jit(solution)/shard_map/finish/pallas_call | solution.py:371

commit v5 on v4

--- a/solution.py
+++ b/solution.py
@@ -50,15 +50,19 @@
     return ref.at[slot, pl.ds(row, 16), pl.ds(column, TILE)]
 
 
-def merged(length, latent, rope, fresh, fresh_rope):
+def placed_new(length, fresh, fresh_rope):
     row = lax.broadcasted_iota(jnp.int32, (ROWS, STEPS), 0)
     step = lax.broadcasted_iota(jnp.int32, (ROWS, STEPS), 1)
     placed = jnp.where(row - length == step, 1.0, 0.0).astype(jnp.bfloat16)
-    added = jnp.dot(placed, fresh, preferred_element_type=jnp.float32).astype(jnp.bfloat16)
-    position = lax.broadcasted_iota(jnp.int32, (ROWS, LATENT), 0)
+    added = jnp.dot(placed, fresh, preferred_element_type=jnp.float32)
     added_rope = lax.dot_general(
         fresh_rope, placed, (((0,), (1,)), ((), ())), preferred_element_type=jnp.float32
-    ).astype(jnp.bfloat16)
+    )
+    return added.astype(jnp.bfloat16), added_rope.astype(jnp.bfloat16)
+
+
+def merged(length, latent, rope, added, added_rope):
+    position = lax.broadcasted_iota(jnp.int32, (ROWS, LATENT), 0)
     position_rope = lax.broadcasted_iota(jnp.int32, (ROPE, ROWS), 1)
     return (
         jnp.where(position < length, latent, added),
@@ -72,13 +76,14 @@
 
 def attention_of(length, keys_ref, keys_rope_ref, q, q_rope, first=0):
     steps = q.shape[0]
-    shape = (steps, HEADS, ROWS)
-    seen = lax.broadcasted_iota(jnp.int32, shape, 2) <= length + first + lax.broadcasted_iota(jnp.int32, shape, 0)
+    shape = (steps * HEADS, ROWS)
+    step = first + lax.broadcasted_iota(jnp.int32, shape, 0) // HEADS
+    seen = lax.broadcasted_iota(jnp.int32, shape, 1) - step <= length
     scores = lax.dot_general(
         q.reshape(steps * HEADS, LATENT), keys_ref[...], (((1,), (1,)), ((), ())),
         preferred_element_type=jnp.float32,
     ) + jnp.dot(q_rope, keys_rope_ref[...], preferred_element_type=jnp.float32)
-    scores = jnp.where(seen.reshape(steps * HEADS, ROWS), scores * LOG2E_SCALE, -jnp.inf)
+    scores = jnp.where(seen, scores * LOG2E_SCALE, -jnp.inf)
     raised = jnp.exp2(scores - jnp.max(scores, axis=1, keepdims=True))
     total = jnp.sum(raised, axis=1, keepdims=True)
     result = jnp.dot(raised.astype(jnp.bfloat16), keys_ref[...], preferred_element_type=jnp.float32)
@@ -86,13 +91,14 @@
 
 
 def exchange_kernel(
-    dest_ref, length_ref, latent_ref, rope_ref, q_ref, q_rope_ref, new_ref, new_rope_ref,
+    dest_hbm, length_hbm, latent_ref, rope_ref, q_ref, q_rope_ref, new_hbm, new_rope_hbm,
     out_latent, out_rope, out_early, out_moved, out_moved_rope, out_q, out_q_rope,
+    out_added, out_added_rope, out_length,
     held, staged, held_rope, staged_rope,
     q_early, q_rope_all, q_turned, arrived, arrived_rope, early, moved, moved_rope,
     send_one, recv_one, send_two, recv_two,
     send_one_rope, recv_one_rope, send_two_rope, recv_two_rope,
-    load_sem, store_sem,
+    load_sem, store_sem, dest_ref, length_ref, new_ref, new_rope_ref, added, added_rope, length_row, small_sem,
 ):
     me = lax.axis_index("dp")
     place = rope_place(me)
@@ -102,6 +108,14 @@
     def _(k):
         pl.semaphore_signal(barrier, inc=1, device_id={"dp": shifted(me, k)}, device_id_type=MESH)
 
+    small = [
+        pltpu.make_async_copy(source, target, small_sem.at[i])
+        for i, (source, target) in enumerate(
+            ((dest_hbm, dest_ref), (length_hbm, length_ref), (new_hbm, new_ref), (new_rope_hbm, new_rope_ref))
+        )
+    ]
+    for copy in small:
+        copy.start()
     pl.semaphore_wait(barrier, RANKS - 1)
 
     def send_rope(slot):
@@ -173,6 +187,8 @@
                     device_id={"dp": peer}, device_id_type=MESH,
                 ).start()
 
+    for copy in small:
+        copy.wait()
     for slot in range(SLOTS):
         pltpu.make_async_copy(held[slot], held[slot], recv_one.at[slot]).wait()
 
@@ -216,6 +232,16 @@
     q_turned[...] = turned(q_rope_all[:, EARLY])
     store_turned = pltpu.make_async_copy(q_turned, out_q_rope, load_sem.at[5])
     store_turned.start()
+    last_length = length_ref[dest_ref[me * SLOTS + EARLY] * SLOTS + EARLY]
+    added[...], added_rope[...] = placed_new(last_length, new_ref[:, EARLY, :], new_rope_ref[:, EARLY, :])
+    length_row[...] = jnp.full((8, TILE), last_length, jnp.int32)
+    last = [
+        pltpu.make_async_copy(added, out_added, load_sem.at[6]),
+        pltpu.make_async_copy(added_rope, out_added_rope, load_sem.at[7]),
+        pltpu.make_async_copy(length_row, out_length, load_sem.at[8]),
+    ]
+    for copy in last:
+        copy.start()
     for slot in range(EARLY):
         arrive(slot)
         load = pltpu.make_async_copy(out_latent.at[slot], arrived, load_sem.at[2])
@@ -226,7 +252,8 @@
         load_rope.wait()
         length = length_ref[dest_ref[me * SLOTS + slot] * SLOTS + slot]
         moved[slot], moved_rope[slot] = merged(
-            length, arrived[...], arrived_rope[...], new_ref[:, slot, :], new_rope_ref[:, slot, :]
+            length, arrived[...], arrived_rope[...],
+            *placed_new(length, new_ref[:, slot, :], new_rope_ref[:, slot, :]),
         )
         early[slot] = attention_of(
             length, moved.at[slot], moved_rope.at[slot], q_early[:, slot], turned(q_rope_all[:, slot])
@@ -252,6 +279,8 @@
 
     load_last.wait()
     store_turned.wait()
+    for copy in last:
+        copy.wait()
     for slot in range(EARLY):
         for copy in stores(slot):
             copy.wait()
@@ -271,7 +300,6 @@
 
 HBM = pl.BlockSpec(memory_space=pltpu.HBM)
 ANY = pl.BlockSpec(memory_space=pl.ANY)
-SMEM = pl.BlockSpec(memory_space=pltpu.SMEM)
 VMEM = pl.BlockSpec(memory_space=pltpu.VMEM)
 
 
@@ -291,9 +319,10 @@
             buffer(SLOTS, ROWS, LATENT), buffer(SLOTS, ROPE, ROWS),
             buffer(EARLY, STEPS, HEADS, LATENT), buffer(EARLY, ROWS, LATENT), buffer(EARLY, ROPE, ROWS),
             buffer(STEPS, HEADS, LATENT), buffer(STEPS * HEADS, ROPE),
-        ),
-        in_specs=[SMEM, SMEM, HBM, HBM, HBM, HBM, VMEM, VMEM],
-        out_specs=(ANY,) * 7,
+            buffer(ROWS, LATENT), buffer(ROPE, ROWS), pltpu.VMEM((8, TILE), jnp.int32),
+        ),
+        in_specs=[HBM] * 8,
+        out_specs=(ANY,) * 10,
         scratch_shapes=[
             (buffer(RANKS, PIECE_ROWS, TILE),) * SLOTS,
             buffer(SLOTS, RANKS, PIECE_ROWS, TILE),
@@ -305,7 +334,10 @@
             buffer(EARLY, STEPS, HEADS, LATENT), buffer(EARLY, ROWS, LATENT), buffer(EARLY, ROPE, ROWS),
             dma((SLOTS,)), dma((SLOTS,)), dma((SLOTS,)), dma((SLOTS,)),
             dma((SLOTS,)), dma((2,)), dma((2,)), dma((SLOTS,)),
-            dma((6,)), dma((3, EARLY)),
+            dma((9,)), dma((3, EARLY)),
+            pltpu.SMEM(req_dest.shape, jnp.int32), pltpu.SMEM(req_length.shape, jnp.int32),
+            buffer(*new_latent.shape), buffer(*new_rope.shape),
+            buffer(ROWS, LATENT), buffer(ROPE, ROWS), pltpu.VMEM((8, TILE), jnp.int32), dma((4,)),
         ],
         compiler_params=pltpu.CompilerParams(
             collective_id=0, has_side_effects=True, vmem_limit_bytes=32 * 2**20
@@ -318,18 +350,11 @@
 
 
 def finish_kernel(
-    dest_ref, length_ref, latent_ref, rope_ref, early_ref, moved_ref, moved_rope_ref,
-    q, q_rope, new_ref, new_rope_ref,
+    latent_ref, rope_ref, early_ref, moved_ref, moved_rope_ref, q, q_rope, added, added_rope, length_ref,
     out_ref, out_moved, out_moved_rope,
-    latent, rope, result, keys, keys_rope, load_sem, store_sem,
+    result, keys, keys_rope, store_sem,
 ):
     slot = EARLY
-    loads = [
-        pltpu.make_async_copy(latent_ref.at[slot], latent, load_sem.at[0]),
-        pltpu.make_async_copy(rope_ref.at[slot], rope, load_sem.at[1]),
-    ]
-    for copy in loads:
-        copy.start()
     copies = [
         pltpu.make_async_copy(early_ref.at[k], out_ref.at[:, k], store_sem.at[k]) for k in range(EARLY)
     ] + [
@@ -338,13 +363,8 @@
     ]
     for copy in copies:
         copy.start()
-    me = lax.axis_index("dp")
-    length = length_ref[dest_ref[me * SLOTS + slot] * SLOTS + slot]
-    loads[0].wait()
-    loads[1].wait()
-    keys[...], keys_rope[...] = merged(
-        length, latent[...], rope[...], new_ref[:, slot, :], new_rope_ref[:, slot, :]
-    )
+    length = length_ref[:1, :1]
+    keys[...], keys_rope[...] = merged(length, latent_ref[slot], rope_ref[slot], added[...], added_rope[...])
     half = STEPS // 2
     own = [
         pltpu.make_async_copy(keys, out_moved.at[slot], store_sem.at[EARLY + 2]),
@@ -366,26 +386,24 @@
         copy.wait()
 
 
-def finish(req_dest, req_length, exchanged, new_latent, new_rope):
+def finish(exchanged):
     dma = pltpu.SemaphoreType.DMA
     return pl.pallas_call(
         finish_kernel,
         out_shape=(
             like(STEPS, SLOTS, HEADS, LATENT), like(SLOTS, ROWS, LATENT), like(SLOTS, ROPE, ROWS),
         ),
-        in_specs=[SMEM, SMEM] + [ANY] * 5 + [VMEM] * 4,
+        in_specs=[VMEM] * 2 + [ANY] * 3 + [VMEM] * 5,
         out_specs=(HBM,) * 3,
         scratch_shapes=[
-            buffer(ROWS, LATENT), buffer(ROPE, ROWS),
-            buffer(STEPS, HEADS, LATENT), buffer(ROWS, LATENT), buffer(ROPE, ROWS),
-            dma((2,)), dma((EARLY + 6,)),
+            buffer(STEPS, HEADS, LATENT), buffer(ROWS, LATENT), buffer(ROPE, ROWS), dma((EARLY + 6,)),
         ],
         compiler_params=pltpu.CompilerParams(vmem_limit_bytes=20 * 2**20),
         cost_estimate=pl.CostEstimate(
             flops=900_000_000, bytes_accessed=12 * 2**20, transcendentals=400_000
         ),
         name="finish",
-    )(req_dest, req_length, *exchanged, new_latent, new_rope)
+    )(*exchanged)
 
 
 def body(latent_cache, rope_cache, q_latent, q_rope, new_latent, new_rope, req_length, req_dest):
@@ -393,7 +411,7 @@
     latent_cache, rope_cache, req_dest, req_length = map(in_hbm, (latent_cache, rope_cache, req_dest, req_length))
     queries = tuple(map(in_hbm, (q_latent, q_rope, new_latent, new_rope)))
     exchanged = exchange(req_dest, req_length, latent_cache, rope_cache, *queries)
-    return finish(req_dest, req_length, exchanged, *queries[2:])
+    return finish(exchanged)
 
 
 def solution(mesh):

time: 95.9 us -> 94 us (0.980)
  Pallas kernels: 95.1 us -> 93.3 us
    pallas_call x1, Pallas kernels: 3.92 us -> 2.83 us  [finish(): pl.pallas_call(finish_kernel, out_shape=(like(STEPS, SLOTS, HEADS, LATENT...]
where the time goes in v5:
time: 94 us; the launch traced here: 93.9 us
  Pallas kernels  93.3 us (99%)
    pallas_call x1, Pallas kernels, exchange(): pl.pallas_call(exchange_kernel, out_shape=(buffer(SLOTS, ROWS, LATENT), b...  90.4 us
    pallas_call x1, Pallas kernels, finish(): pl.pallas_call(finish_kernel, out_shape=(like(STEPS, SLOTS, HEADS, LATENT...  2.83 us

profile of v5, /device:TPU:1, one launch (start us, length us, event | category | flops | bytes accessed | tf_op | source)
XLA Modules:
  0.0 93.9 jit_solution(7925716401356555069)
XLA Ops:
  0.6 90.4 %exchange.1 = (bf16[4,384,512]{2,1,0:T(8,128)(2,1)S(1)}, bf16[4,64,384]{2,1,0:T(8,128)(2,1)S(1)}, bf16[3,8,128,512]{3,2,1,0:T(8,128)(2,1)S(1)}, bf16[3,384,512]{...) custom-call(s32[128]{0:T(128)} %dest_hbm.1, ...), custom_call_target="tpu_custom_call" | custom-call | flops 2600000000 | bytes 16777216 | tf_op jit(solution)/shard_map/exchange/pallas_call | solution.py:316
  91.1 2.8 %finish.1 = (bf16[8,4,128,512]{3,2,1,0:T(8,128)(2,1)}, bf16[4,384,512]{2,1,0:T(8,128)(2,1)}, bf16[4,64,384]{2,1,0:T(8,128)(2,1)}) custom-call(bf16[4,384,512]{2,1,0:T(8,128)(2,1)S(1)} %get-tuple-element.13.latent_ref, bf16[4,64,384]{2,1,0:T(8,128)(2,1)S(1)} %get-tuple-element.14.rope_ref, bf16[3,8,128,512]{3,2,1,0:T(8,128)(2,1)S(1)} %get-tuple-element.15.early_ref, ...), custom_call_target="tpu_custom_call" | custom-call | flops 900000000 | bytes 12582912 | tf_op jit(solution)/shard_map/finish/pallas_call | solution.py:391

commit v6 on v5

--- a/solution.py
+++ b/solution.py
@@ -74,7 +74,7 @@
     return jnp.concatenate([q_rope[t].T for t in range(STEPS)], axis=0)
 
 
-def attention_of(length, keys_ref, keys_rope_ref, q, q_rope, first=0):
+def scores_of(length, keys_ref, keys_rope_ref, q, q_rope, first=0):
     steps = q.shape[0]
     shape = (steps * HEADS, ROWS)
     step = first + lax.broadcasted_iota(jnp.int32, shape, 0) // HEADS
@@ -83,11 +83,18 @@
         q.reshape(steps * HEADS, LATENT), keys_ref[...], (((1,), (1,)), ((), ())),
         preferred_element_type=jnp.float32,
     ) + jnp.dot(q_rope, keys_rope_ref[...], preferred_element_type=jnp.float32)
-    scores = jnp.where(seen, scores * LOG2E_SCALE, -jnp.inf)
+    return jnp.where(seen, scores * LOG2E_SCALE, -jnp.inf)
+
+
+def weighted(scores, keys_ref):
     raised = jnp.exp2(scores - jnp.max(scores, axis=1, keepdims=True))
     total = jnp.sum(raised, axis=1, keepdims=True)
     result = jnp.dot(raised.astype(jnp.bfloat16), keys_ref[...], preferred_element_type=jnp.float32)
-    return (result * (1.0 / total)).astype(jnp.bfloat16).reshape(steps, HEADS, LATENT)
+    return (result * (1.0 / total)).astype(jnp.bfloat16).reshape(-1, HEADS, LATENT)
+
+
+def attention_of(length, keys_ref, keys_rope_ref, q, q_rope):
+    return weighted(scores_of(length, keys_ref, keys_rope_ref, q, q_rope), keys_ref)
 
 
 def exchange_kernel(
@@ -142,6 +149,7 @@
                         ).start()
 
     for slot in range(SLOTS):
+        send_rope(slot)
         pltpu.make_async_copy(
             latent_piece(latent_ref, slot, me), held[slot].at[me], recv_one.at[slot]
         ).start()
@@ -155,8 +163,6 @@
                 device_id={"dp": peer}, device_id_type=MESH,
             ).start()
 
-        send_rope(slot)
-
     load_q = pltpu.make_async_copy(q_ref.at[:, pl.ds(0, EARLY)], q_early, load_sem.at[0])
     load_q_rope = pltpu.make_async_copy(q_rope_ref, q_rope_all, load_sem.at[1])
     load_last = pltpu.make_async_copy(q_ref.at[:, EARLY], out_q, load_sem.at[4])
@@ -190,6 +196,12 @@
     for copy in small:
         copy.wait()
     for slot in range(SLOTS):
+        for u in range(2):
+            first, last = slot * ROPE_UNITS - RANKS * u, slot * ROPE_UNITS + ROPE_UNITS - RANKS * u
+            first, last = max(first, 0), min(last, RANKS if u == 0 else 16)
+            if first < last:
+                pl.when((place >= first) & (place < last))(lambda u=u: forward_rope(u))
+
         pltpu.make_async_copy(held[slot], held[slot], recv_one.at[slot]).wait()
 
         @pl.loop(0, RANKS)
@@ -209,12 +221,6 @@
                     source, target, send_two.at[slot], recv_two.at[slot],
                     device_id={"dp": peer}, device_id_type=MESH,
                 ).start()
-
-        for u in range(2):
-            first, last = slot * ROPE_UNITS - RANKS * u, slot * ROPE_UNITS + ROPE_UNITS - RANKS * u
-            first, last = max(first, 0), min(last, RANKS if u == 0 else 16)
-            if first < last:
-                pl.when((place >= first) & (place < last))(lambda u=u: forward_rope(u))
 
     def arrive(slot):
         pltpu.make_async_copy(out_latent.at[slot], out_latent.at[slot], recv_two.at[slot]).wait()
@@ -365,23 +371,25 @@
         copy.start()
     length = length_ref[:1, :1]
     keys[...], keys_rope[...] = merged(length, latent_ref[slot], rope_ref[slot], added[...], added_rope[...])
-    half = STEPS // 2
+    part = STEPS // 2
     own = [
         pltpu.make_async_copy(keys, out_moved.at[slot], store_sem.at[EARLY + 2]),
         pltpu.make_async_copy(keys_rope, out_moved_rope.at[slot], store_sem.at[EARLY + 3]),
-    ] + [
-        pltpu.make_async_copy(
-            result.at[pl.ds(first, half)], out_ref.at[pl.ds(first, half), slot],
-            store_sem.at[EARLY + 4 + first // half],
-        )
-        for first in (0, half)
     ]
     own[0].start()
     own[1].start()
-    result[:half] = attention_of(length, keys, keys_rope, q[:half], q_rope[: half * HEADS])
-    own[2].start()
-    result[half:] = attention_of(length, keys, keys_rope, q[half:], q_rope[half * HEADS :], half)
-    own[3].start()
+    scores = [
+        scores_of(length, keys, keys_rope, q[k : k + part], q_rope[k * HEADS : (k + part) * HEADS], k)
+        for k in range(0, STEPS, part)
+    ]
+    for i, k in enumerate(range(0, STEPS, part)):
+        result[k : k + part] = weighted(scores[i], keys)
+        own.append(
+            pltpu.make_async_copy(
+                result.at[pl.ds(k, part)], out_ref.at[pl.ds(k, part), slot], store_sem.at[EARLY + 4 + i]
+            )
+        )
+        own[-1].start()
     for copy in copies + own:
         copy.wait()
 

time: 94 us -> 93.5 us (level)
  no operation moved by 1% of the time
where the time goes in v6:
time: 93.5 us; the launch traced here: 93.3 us
  Pallas kernels  92.6 us (99%)
    pallas_call x1, Pallas kernels, exchange(): pl.pallas_call(exchange_kernel, out_shape=(buffer(SLOTS, ROWS, LATENT), b...  90 us
    pallas_call x1, Pallas kernels, finish(): pl.pallas_call(finish_kernel, out_shape=(like(STEPS, SLOTS, HEADS, LATENT...  2.64 us

profile of v6, /device:TPU:1, one launch (start us, length us, event | category | flops | bytes accessed | tf_op | source)
XLA Modules:
  0.0 93.3 jit_solution(9836097154889011925)
XLA Ops:
  0.6 90.0 %exchange.1 = (bf16[4,384,512]{2,1,0:T(8,128)(2,1)S(1)}, bf16[4,64,384]{2,1,0:T(8,128)(2,1)S(1)}, bf16[3,8,128,512]{3,2,1,0:T(8,128)(2,1)S(1)}, bf16[3,384,512]{...) custom-call(s32[128]{0:T(128)} %dest_hbm.1, ...), custom_call_target="tpu_custom_call" | custom-call | flops 2600000000 | bytes 16777216 | tf_op jit(solution)/shard_map/exchange/pallas_call | solution.py:322
  90.6 2.6 %finish.1 = (bf16[8,4,128,512]{3,2,1,0:T(8,128)(2,1)}, bf16[4,384,512]{2,1,0:T(8,128)(2,1)}, bf16[4,64,384]{2,1,0:T(8,128)(2,1)}) custom-call(bf16[4,384,512]{2,1,0:T(8,128)(2,1)S(1)} %get-tuple-element.13.latent_ref, bf16[4,64,384]{2,1,0:T(8,128)(2,1)S(1)} %get-tuple-element.14.rope_ref, bf16[3,8,128,512]{3,2,1,0:T(8,128)(2,1)S(1)} %get-tuple-element.15.early_ref, ...), custom_call_target="tpu_custom_call" | custom-call | flops 900000000 | bytes 12582912 | tf_op jit(solution)/shard_map/finish/pallas_call | solution.py:399

commit v7 on v6

--- a/solution.py
+++ b/solution.py
@@ -18,7 +18,10 @@
 HEADS = 128
 PIECE_ROWS = 48
 TILE = 128
-ROPE_UNITS = 12
+SENT_ROWS = 368
+SHORT_ROWS = 32
+ROPE_UNITS = 14
+TWICE = 24
 EARLY = 3
 LOG2E_SCALE = 192.0 ** (-0.5) * math.log2(math.e)
 
@@ -38,10 +41,31 @@
     return y * RING + 2 * z + (y + half) % 2
 
 
-def latent_piece(ref, slot, piece):
+def piece_of(rank, slot):
+    return rank if slot % 2 == 0 else rank + 4 - 8 * (rank // 4 % 2)
+
+
+def latent_piece(ref, slot, piece, rows):
     row = pl.multiple_of(piece // 4 * PIECE_ROWS, PIECE_ROWS)
     column = pl.multiple_of(piece % 4 * TILE, TILE)
-    return ref.at[slot, pl.ds(row, PIECE_ROWS), pl.ds(column, TILE)]
+    return ref.at[slot, pl.ds(row, rows), pl.ds(column, TILE)]
+
+
+def by_length(piece, action):
+    pl.when(piece // 4 == 7)(lambda: action(SHORT_ROWS))
+    pl.when(piece // 4 != 7)(lambda: action(PIECE_ROWS))
+
+
+def packed(rows):
+    wide = rows.astype(jnp.float32)
+    return jnp.concatenate([wide[:, k * TILE : (k + 1) * TILE] for k in range(4)], axis=0).astype(jnp.bfloat16)
+
+
+def unpacked(latent, units):
+    wide = units.astype(jnp.float32)
+    rows = jnp.concatenate([wide[8 * k : 8 * k + 8] for k in range(4)], axis=1)
+    rows = jnp.concatenate([rows, jnp.zeros_like(rows)], axis=0).astype(jnp.bfloat16)
+    return jnp.concatenate([latent, rows], axis=0)
 
 
 def rope_unit(ref, slot, unit):
@@ -106,6 +130,7 @@
     send_one, recv_one, send_two, recv_two,
     send_one_rope, recv_one_rope, send_two_rope, recv_two_rope,
     load_sem, store_sem, dest_ref, length_ref, new_ref, new_rope_ref, added, added_rope, length_row, small_sem,
+    units, tail, send_one_short,
 ):
     me = lax.axis_index("dp")
     place = rope_place(me)
@@ -123,6 +148,10 @@
     ]
     for copy in small:
         copy.start()
+    load_units = pltpu.make_async_copy(rope_ref, units.at[:, :, pl.ds(0, ROWS)], small_sem.at[4])
+    load_tail = pltpu.make_async_copy(latent_ref.at[:, pl.ds(SENT_ROWS, 16)], tail, small_sem.at[5])
+    load_units.start()
+    load_tail.start()
     pl.semaphore_wait(barrier, RANKS - 1)
 
     def send_rope(slot):
@@ -131,7 +160,7 @@
             q = (i + me) % ROPE_UNITS
             unit = slot * ROPE_UNITS + q
             peer, u = rope_rank(unit % RANKS), unit // RANKS
-            source = rope_unit(rope_ref, slot, q)
+            source = rope_unit(units, slot, q)
 
             for w in range(2):
                 if slot * ROPE_UNITS // RANKS <= w <= (slot * ROPE_UNITS + ROPE_UNITS - 1) // RANKS:
@@ -149,19 +178,34 @@
                         ).start()
 
     for slot in range(SLOTS):
+        if slot == 0:
+            load_units.wait()
+            load_tail.wait()
+            for k in range(SLOTS):
+                units[k, 0:32, ROWS : ROWS + TILE] = packed(tail[k, 0:8, :])
         send_rope(slot)
-        pltpu.make_async_copy(
-            latent_piece(latent_ref, slot, me), held[slot].at[me], recv_one.at[slot]
-        ).start()
+
+        def keep(rows):
+            pltpu.make_async_copy(
+                latent_piece(latent_ref, slot, piece_of(me, slot), rows),
+                held[slot].at[me, pl.ds(0, rows)], recv_one.at[slot],
+            ).start()
+
+        by_length(piece_of(me, slot), keep)
 
         @pl.loop(1, RANKS)
         def _(k):
             peer = shifted(me, k)
-            pltpu.make_async_remote_copy(
-                latent_piece(latent_ref, slot, peer), held[slot].at[me],
-                send_one.at[slot], recv_one.at[slot],
-                device_id={"dp": peer}, device_id_type=MESH,
-            ).start()
+            piece = piece_of(peer, slot)
+
+            def send(rows):
+                pltpu.make_async_remote_copy(
+                    latent_piece(latent_ref, slot, piece, rows), held[slot].at[me, pl.ds(0, rows)],
+                    (send_one_short if rows == SHORT_ROWS else send_one).at[slot], recv_one.at[slot],
+                    device_id={"dp": peer}, device_id_type=MESH,
+                ).start()
+
+            by_length(piece, send)
 
     load_q = pltpu.make_async_copy(q_ref.at[:, pl.ds(0, EARLY)], q_early, load_sem.at[0])
     load_q_rope = pltpu.make_async_copy(q_rope_ref, q_rope_all, load_sem.at[1])
@@ -198,33 +242,42 @@
     for slot in range(SLOTS):
         for u in range(2):
             first, last = slot * ROPE_UNITS - RANKS * u, slot * ROPE_UNITS + ROPE_UNITS - RANKS * u
-            first, last = max(first, 0), min(last, RANKS if u == 0 else 16)
+            first, last = max(first, 0), min(last, RANKS if u == 0 else TWICE)
             if first < last:
                 pl.when((place >= first) & (place < last))(lambda u=u: forward_rope(u))
 
-        pltpu.make_async_copy(held[slot], held[slot], recv_one.at[slot]).wait()
-
-        @pl.loop(0, RANKS)
-        def _(k):
-            peer = shifted(me, k)
-            origin = dest_ref[peer * SLOTS + slot]
-            staged[slot, peer] = held[slot][origin]
-            source, target = staged.at[slot, peer], latent_piece(out_latent, slot, me)
-
-            @pl.when(k == 0)
-            def _():
-                pltpu.make_async_copy(source, target, recv_two.at[slot]).start()
-
-            @pl.when(k != 0)
-            def _():
-                pltpu.make_async_remote_copy(
-                    source, target, send_two.at[slot], recv_two.at[slot],
-                    device_id={"dp": peer}, device_id_type=MESH,
-                ).start()
+        mine = piece_of(me, slot)
+
+        def forward(rows):
+            part = held[slot].at[:, pl.ds(0, rows)]
+            pltpu.make_async_copy(part, part, recv_one.at[slot]).wait()
+
+            @pl.loop(0, RANKS)
+            def _(k):
+                peer = shifted(me, k)
+                origin = dest_ref[peer * SLOTS + slot]
+                staged[slot, peer, 0:rows] = held[slot][origin, 0:rows]
+                source = staged.at[slot, peer, pl.ds(0, rows)]
+                target = latent_piece(out_latent, slot, mine, rows)
+
+                @pl.when(k == 0)
+                def _():
+                    pltpu.make_async_copy(source, target, recv_two.at[slot]).start()
+
+                @pl.when(k != 0)
+                def _():
+                    pltpu.make_async_remote_copy(
+                        source, target, send_two.at[slot], recv_two.at[slot],
+                        device_id={"dp": peer}, device_id_type=MESH,
+                    ).start()
+
+        by_length(mine, forward)
 
     def arrive(slot):
-        pltpu.make_async_copy(out_latent.at[slot], out_latent.at[slot], recv_two.at[slot]).wait()
-        pltpu.make_async_copy(out_rope.at[slot], out_rope.at[slot], recv_two_rope.at[slot]).wait()
+        rows = out_latent.at[slot, pl.ds(0, SENT_ROWS)]
+        pltpu.make_async_copy(rows, rows, recv_two.at[slot]).wait()
+        part = staged_rope.at[0, pl.ds(0, ROPE_UNITS)]
+        pltpu.make_async_copy(part, part, recv_two_rope.at[slot]).wait()
 
     def stores(slot):
         return [
@@ -250,7 +303,7 @@
         copy.start()
     for slot in range(EARLY):
         arrive(slot)
-        load = pltpu.make_async_copy(out_latent.at[slot], arrived, load_sem.at[2])
+        load = pltpu.make_async_copy(out_latent.at[slot, pl.ds(0, SENT_ROWS)], arrived, load_sem.at[2])
         load_rope = pltpu.make_async_copy(out_rope.at[slot], arrived_rope, load_sem.at[3])
         load.start()
         load_rope.start()
@@ -258,7 +311,7 @@
         load_rope.wait()
         length = length_ref[dest_ref[me * SLOTS + slot] * SLOTS + slot]
         moved[slot], moved_rope[slot] = merged(
-            length, arrived[...], arrived_rope[...],
+            length, unpacked(arrived[...], arrived_rope[0:32, ROWS:]), arrived_rope[:, :ROWS],
             *placed_new(length, new_ref[:, slot, :], new_rope_ref[:, slot, :]),
         )
         early[slot] = attention_of(
@@ -269,9 +322,16 @@
 
     others = pl.ds(0, RANKS - 1)
     for slot in range(SLOTS):
-        pltpu.make_async_copy(held[slot].at[others], held[slot].at[others], send_one.at[slot]).wait()
+        def sent(rows):
+            short = 3 if rows == SHORT_ROWS else 4
+            part = held[slot].at[pl.ds(0, RANKS - 1 - short)]
+            pltpu.make_async_copy(part, part, send_one.at[slot]).wait()
+            part = held[slot].at[pl.ds(0, short), pl.ds(0, SHORT_ROWS)]
+            pltpu.make_async_copy(part, part, send_one_short.at[slot]).wait()
+
+        by_length(piece_of(me, slot), sent)
         own = place // ROPE_UNITS == slot
-        own |= (place < 16) & ((place + RANKS) // ROPE_UNITS == slot)
+        own |= (place < TWICE) & ((place + RANKS) // ROPE_UNITS == slot)
 
         @pl.when(own)
         def _():
@@ -291,12 +351,16 @@
         for copy in stores(slot):
             copy.wait()
     for slot in range(SLOTS):
-        pltpu.make_async_copy(staged.at[slot, others], staged.at[slot, others], send_two.at[slot]).wait()
+        def sent(rows):
+            part = staged.at[slot, others, pl.ds(0, rows)]
+            pltpu.make_async_copy(part, part, send_two.at[slot]).wait()
+
+        by_length(piece_of(me, slot), sent)
 
     rest = staged_rope.at[0, others]
     pltpu.make_async_copy(rest, rest, send_two_rope.at[0]).wait()
 
-    @pl.when(place < 16)
+    @pl.when(place < TWICE)
     def _():
         pltpu.make_async_copy(rest, rest, send_two_rope.at[1]).wait()
 
@@ -322,7 +386,7 @@
     return pl.pallas_call(
         exchange_kernel,
         out_shape=(
-            buffer(SLOTS, ROWS, LATENT), buffer(SLOTS, ROPE, ROWS),
+            buffer(SLOTS, ROWS, LATENT), buffer(SLOTS, ROPE, ROWS + TILE),
             buffer(EARLY, STEPS, HEADS, LATENT), buffer(EARLY, ROWS, LATENT), buffer(EARLY, ROPE, ROWS),
             buffer(STEPS, HEADS, LATENT), buffer(STEPS * HEADS, ROPE),
             buffer(ROWS, LATENT), buffer(ROPE, ROWS), pltpu.VMEM((8, TILE), jnp.int32),
@@ -336,14 +400,15 @@
             buffer(2, RANKS, 16, TILE),
             buffer(STEPS, EARLY, HEADS, LATENT), buffer(STEPS, SLOTS, ROPE, HEADS),
             buffer(STEPS * HEADS, ROPE),
-            buffer(ROWS, LATENT), buffer(ROPE, ROWS),
+            buffer(SENT_ROWS, LATENT), buffer(ROPE, ROWS + TILE),
             buffer(EARLY, STEPS, HEADS, LATENT), buffer(EARLY, ROWS, LATENT), buffer(EARLY, ROPE, ROWS),
             dma((SLOTS,)), dma((SLOTS,)), dma((SLOTS,)), dma((SLOTS,)),
             dma((SLOTS,)), dma((2,)), dma((2,)), dma((SLOTS,)),
             dma((9,)), dma((3, EARLY)),
             pltpu.SMEM(req_dest.shape, jnp.int32), pltpu.SMEM(req_length.shape, jnp.int32),
             buffer(*new_latent.shape), buffer(*new_rope.shape),
-            buffer(ROWS, LATENT), buffer(ROPE, ROWS), pltpu.VMEM((8, TILE), jnp.int32), dma((4,)),
+            buffer(ROWS, LATENT), buffer(ROPE, ROWS), pltpu.VMEM((8, TILE), jnp.int32), dma((6,)),
+            buffer(SLOTS, ROPE, ROWS + TILE), buffer(SLOTS, 16, LATENT), dma((SLOTS,)),
         ],
         compiler_params=pltpu.CompilerParams(
             collective_id=0, has_side_effects=True, vmem_limit_bytes=32 * 2**20
@@ -370,7 +435,10 @@
     for copy in copies:
         copy.start()
     length = length_ref[:1, :1]
-    keys[...], keys_rope[...] = merged(length, latent_ref[slot], rope_ref[slot], added[...], added_rope[...])
+    keys[...], keys_rope[...] = merged(
+        length, unpacked(latent_ref[slot, :SENT_ROWS], rope_ref[slot, 0:32, ROWS:]), rope_ref[slot, :, :ROWS],
+        added[...], added_rope[...],
+    )
     part = STEPS // 2
     own = [
         pltpu.make_async_copy(keys, out_moved.at[slot], store_sem.at[EARLY + 2]),

time: 93.5 us -> 93.5 us (level)
  no operation moved by 1% of the time
where the time goes in v7:
time: 93.5 us
  Pallas kernels  92.8 us (99%)
    pallas_call x1, Pallas kernels, exchange(): pl.pallas_call(exchange_kernel, out_shape=(buffer(SLOTS, ROWS, LATENT), b...  90.1 us
    pallas_call x1, Pallas kernels, finish(): pl.pallas_call(finish_kernel, out_shape=(like(STEPS, SLOTS, HEADS, LATENT...  2.71 us

profile of v7, /device:TPU:1, one launch (start us, length us, event | category | flops | bytes accessed | tf_op | source)
XLA Modules:
  0.0 93.5 jit_solution(9034262558790269784)
XLA Ops:
  0.6 90.1 %exchange.1 = (bf16[4,384,512]{2,1,0:T(8,128)(2,1)S(1)}, bf16[4,64,512]{2,1,0:T(8,128)(2,1)S(1)}, bf16[3,8,128,512]{3,2,1,0:T(8,128)(2,1)S(1)}, bf16[3,384,512]{...) custom-call(s32[128]{0:T(128)} %dest_hbm.1, ...), custom_call_target="tpu_custom_call" | custom-call | flops 2600000000 | bytes 16777216 | tf_op jit(solution)/shard_map/exchange/pallas_call | solution.py:386
  90.7 2.7 %finish.1 = (bf16[8,4,128,512]{3,2,1,0:T(8,128)(2,1)}, bf16[4,384,512]{2,1,0:T(8,128)(2,1)}, bf16[4,64,384]{2,1,0:T(8,128)(2,1)}) custom-call(bf16[4,384,512]{2,1,0:T(8,128)(2,1)S(1)} %get-tuple-element.13.latent_ref, bf16[4,64,512]{2,1,0:T(8,128)(2,1)S(1)} %get-tuple-element.14.rope_ref, bf16[3,8,128,512]{3,2,1,0:T(8,128)(2,1)S(1)} %get-tuple-element.15.early_ref, ...), custom_call_target="tpu_custom_call" | custom-call | flops 900000000 | bytes 12582912 | tf_op jit(solution)/shard_map/finish/pallas_call | solution.py:467
